TPU v7x, 128 devices: a whole 4x4x4 slice. The times are simulated.
128 devices in a mesh: col: 64 (over y, z, x), row: 2 (over core).
Axes of the slice: x: 4, y: 4, z: 4, core: 2. Of those that a mesh axis runs over, the one named last changes fastest.
Arguments:
- front: float32 [16384, 16384], P('row', 'col'), as said below
- row_map: int32 [128], replicated, may hold values from 0 to 127, each once
Outputs:
- factored: float32 [16384, 16384], P('row', 'col')
- parent_rows: float32 [16384, 16384], P('row', 'col')
Inputs may be any that keep to these rules, and one draw needn't show every extreme that they name: front is symmetric and positive definite.
All inputs are finite; a program needn't handle non-finite values.
Results may differ from a plain program's by a relative error of at most 0.0003.
Values sent between devices are 32-bit elements; how exact they have to be, the bound alone decides.
No kernel may reach another device: no remote copies, remote signals or barrier semaphores. Data moves between devices by JAX's collectives and lax.ppermute only.
A program may use at most 192 MiB of HBM per device.

v0:
```python
import jax
import jax.numpy as jnp
from jax import lax
from jax.sharding import PartitionSpec as P

B = 128
PANELS = 6


def from_root(block, axis, holder):
    block = jnp.where(lax.axis_index(axis) == holder, block, jnp.zeros_like(block))
    return lax.psum(block, axis)


def partner(x, axis, distance):
    return lax.ppermute(x, axis, [(i, i ^ 1 << distance) for i in range(lax.axis_size(axis))])


def per_device(front, row_map):
    rows_here, cols_here = front.shape
    row_start = lax.axis_index("row") * rows_here
    col_index = lax.axis_index("col")
    col_start = col_index * cols_here
    global_row = row_start + lax.broadcasted_iota(jnp.int32, (rows_here, 1), 0)
    global_col = col_start + lax.broadcasted_iota(jnp.int32, (1, cols_here), 1)
    matrix = front
    no_skip = jnp.zeros((1, 1), jnp.bool_)
    for panel in range(PANELS):
        pivot_start = panel * B
        offset = pivot_start % cols_here
        columns = matrix[:, offset : offset + B]
        root_row = pivot_start // rows_here
        factor_offset = pivot_start % rows_here
        diag_block = from_root(columns[factor_offset : factor_offset + B], "row", root_row)
        cholesky_block = jnp.linalg.cholesky(diag_block)
        solved = jax.scipy.linalg.solve_triangular(cholesky_block, columns.T, lower=True).T
        solved = jnp.where(global_row >= pivot_start, solved, 0.0)
        owner_col = pivot_start // cols_here
        factor_halves = from_root(solved, "col", owner_col)
        inside = (col_start >= row_start) & (col_start < row_start + rows_here)
        local_offset = jnp.clip(col_start - row_start, 0, rows_here - cols_here)
        own_rows = lax.dynamic_slice_in_dim(factor_halves, local_offset, cols_here, 0)
        other_rows = partner(own_rows, "row", 0)
        factor_col_rows = jnp.where(inside, own_rows, other_rows)
        finish_matrix = matrix
        pivot_end = pivot_start + B
        product = jnp.dot(factor_halves, factor_col_rows.T, precision=lax.Precision.HIGHEST)
        trail_mask = (
            (global_row >= pivot_end) & (global_col >= pivot_end) & jnp.logical_not(no_skip)
        )
        finish_matrix = finish_matrix - jnp.where(trail_mask, product, 0.0)
        finish_offset = pivot_start % cols_here
        is_owner = col_index == pivot_start // cols_here
        finish_matrix = finish_matrix.at[:, finish_offset : finish_offset + B].set(
            jnp.where(is_owner, factor_halves, finish_matrix[:, finish_offset : finish_offset + B])
        )
        cleared = (global_row >= pivot_start) & (global_row < pivot_end) & (global_col >= pivot_end)
        matrix = jnp.where(cleared, 0.0, finish_matrix)
    update = jnp.where(global_col >= PANELS * B, matrix, 0.0)
    blocks_here = rows_here // B
    my_blocks = row_start // B + lax.broadcasted_iota(jnp.int32, (blocks_here,), 0)
    shard_rows = lax.all_gather(update, "row", axis=0, tiled=True)
    block_count = shard_rows.shape[0] // B
    selection = (row_map[None, :] == my_blocks[:, None]).astype(jnp.float32)
    parent = jnp.einsum(
        "ij,jbc->ibc",
        selection,
        shard_rows.reshape(block_count, B, cols_here),
        precision=lax.Precision.HIGHEST,
    )
    return (matrix, parent.reshape(rows_here, cols_here))


def solution(mesh):
    placed = (P("row", "col"), P())
    return jax.shard_map(
        per_device,
        mesh=mesh,
        in_specs=placed,
        out_specs=(P("row", "col"), P("row", "col")),
        check_vma=False,
    )
```

profile of v0, /device:TPU:1, one launch (start us, length us, event | category | flops | bytes accessed | tf_op | source)
XLA Modules:
  0.0 1423.7 jit_solution(14517992698855949980)
XLA Ops:
  17.7 27.0 %all-reduce.13.cloned.1.call-done = f32[128,128]{0,1:T(8,128)} async-done(((f32[128,128]{0,1:T(8,128)}), f32[128,128]{0,1:T(8,128)}) %all-reduce.13.cloned.1.call-update) | async-done | bytes 65552 | tf_op jit(solution)/shard_map/psum | solution.py:12
  46.5 11.7 cholesky.104
  59.5 9.8 custom-call.10
  77.6 138.3 %all-reduce.15.cloned.1.call-done = f32[8192,128]{0,1:T(8,128)} async-done(((f32[8192,128]{0,1:T(8,128)}), f32[8192,128]{0,1:T(8,128)}) %all-reduce.15.cloned.1.call-update) | async-done | bytes 4194320 | tf_op jit(solution)/shard_map/psum | solution.py:12
  220.3 10.9 fusion.5
  238.7 21.1 %all-reduce.17.cloned.1.call-done = f32[128,128]{0,1:T(8,128)} async-done(((f32[128,128]{0,1:T(8,128)}), f32[128,128]{0,1:T(8,128)}) %all-reduce.17.cloned.1.call-update) | async-done | bytes 65552 | tf_op jit(solution)/shard_map/psum | solution.py:12
  261.6 11.7 cholesky.115
  292.7 138.2 %all-reduce.19.cloned.1.call-done = f32[8192,128]{0,1:T(8,128)} async-done(((f32[8192,128]{0,1:T(8,128)}), f32[8192,128]{0,1:T(8,128)}) %all-reduce.19.cloned.1.call-update) | async-done | bytes 4194320 | tf_op jit(solution)/shard_map/psum | solution.py:12
  431.9 13.6 collective-permute-start.1
  446.5 11.0 fusion.4
  464.2 20.7 %all-reduce.21.cloned.1.call-done = f32[128,128]{0,1:T(8,128)} async-done(((f32[128,128]{0,1:T(8,128)}), f32[128,128]{0,1:T(8,128)}) %all-reduce.21.cloned.1.call-update) | async-done | bytes 65552 | tf_op jit(solution)/shard_map/psum | solution.py:12
  486.7 11.7 cholesky.126
  517.7 138.4 %all-reduce.23.cloned.1.call-done = f32[8192,128]{0,1:T(8,128)} async-done(((f32[8192,128]{0,1:T(8,128)}), f32[8192,128]{0,1:T(8,128)}) %all-reduce.23.cloned.1.call-update) | async-done | bytes 4194320 | tf_op jit(solution)/shard_map/psum | solution.py:12
  660.5 11.0 fusion.3
  679.4 20.3 %all-reduce.25.cloned.1.call-done = f32[128,128]{0,1:T(8,128)} async-done(((f32[128,128]{0,1:T(8,128)}), f32[128,128]{0,1:T(8,128)}) %all-reduce.25.cloned.1.call-update) | async-done | bytes 65552 | tf_op jit(solution)/shard_map/psum | solution.py:12
  701.5 11.7 cholesky.137
  732.6 138.2 %all-reduce.27.cloned.1.call-done = f32[8192,128]{0,1:T(8,128)} async-done(((f32[8192,128]{0,1:T(8,128)}), f32[8192,128]{0,1:T(8,128)}) %all-reduce.27.cloned.1.call-update) | async-done | bytes 4194320 | tf_op jit(solution)/shard_map/psum | solution.py:12
  875.2 11.0 fusion.2
  892.9 20.7 %all-reduce.29.cloned.1.call-done = f32[128,128]{0,1:T(8,128)} async-done(((f32[128,128]{0,1:T(8,128)}), f32[128,128]{0,1:T(8,128)}) %all-reduce.29.cloned.1.call-update) | async-done | bytes 65552 | tf_op jit(solution)/shard_map/psum | solution.py:12
  915.3 11.7 cholesky.148
  946.4 138.3 %all-reduce.31.cloned.1.call-done = f32[8192,128]{0,1:T(8,128)} async-done(((f32[8192,128]{0,1:T(8,128)}), f32[8192,128]{0,1:T(8,128)}) %all-reduce.31.cloned.1.call-update) | async-done | bytes 4194320 | tf_op jit(solution)/shard_map/psum | solution.py:12
  1089.1 11.0 fusion.1
  1108.1 20.3 %all-reduce.33.cloned.1.call-done = f32[128,128]{0,1:T(8,128)} async-done(((f32[128,128]{0,1:T(8,128)}), f32[128,128]{0,1:T(8,128)}) %all-reduce.33.cloned.1.call-update) | async-done | bytes 65552 | tf_op jit(solution)/shard_map/psum | solution.py:12
  1130.2 11.7 cholesky.159
  1143.2 9.8 custom-call.15
  1161.2 138.2 %all-reduce.35.cloned.1.call-done = f32[8192,128]{0,1:T(8,128)} async-done(((f32[8192,128]{0,1:T(8,128)}), f32[8192,128]{0,1:T(8,128)}) %all-reduce.35.cloned.1.call-update) | async-done | bytes 4194320 | tf_op jit(solution)/shard_map/psum | solution.py:12
  1303.8 15.2 %fusion = f32[8192,256]{0,1:T(8,128)} fusion(f32[8192,256]{0,1:T(8,128)} %copy-done, f32[8192,128]{0,1:T(8,128)} %all-reduce.35.cloned.1.call-done, pred[8192]{0:T(1024)(128)(4,1)S(1)} %get-tuple-element.82, pred[256]{0:T(512)(128)(4,1)S(1)} %fusion.85, f32[256,128]{0,1:T(8,128)S(1)} %constant_dynamic-slice_fusion, ...), kind=kOutput, calls=%fused_computation.1 | convolution fusion | flops 3227549696 | bytes 21242112 | tf_op jit(solution)/shard_map/dot_general | solution.py:47
  1323.8 12.4 broadcast_select_fusion
  1345.7 20.7 %all-gather.2.cloned.1.call-done = f32[16384,256]{0,1:T(8,128)} async-done(((f32[8192,256]{0,1:T(8,128)}), f32[16384,256]{0,1:T(8,128)}) %all-gather.2.cloned.1.call-update) | async-done | bytes 16777232 | tf_op jit(solution)/shard_map/all_gather | solution.py:62
  1366.5 14.1 copy.43
  1380.6 17.8 %copy.34 = f32[128,128,256]{2,0,1:T(8,128)} copy(f32[128,128,256]{1,0,2:T(8,128)} %bitcast.99) | data formatting | bytes 33554432 | tf_op jit(solution)/shard_map/reshape | solution.py:68
  1398.4 10.3 fusion.75
  (147 shorter events, 200.4 us)
Async XLA Ops:
  7.2 37.5 %all-reduce.13.cloned.1.call-start = ((), (), s32[]{:S(2)}) async-start(), calls=%async_computation | async-start | bytes 131072 | tf_op jit(solution)/shard_map/psum | solution.py:12
  17.6 198.3 %all-reduce.15.cloned.1.call-start = ((), (), s32[]{:S(2)}) async-start(), calls=%async_computation.1 | async-start | bytes 8388608 | tf_op jit(solution)/shard_map/psum | solution.py:12
  77.5 182.3 %all-reduce.17.cloned.1.call-start = ((), (), s32[]{:S(2)}) async-start(), calls=%async_computation.2 | async-start | bytes 131072 | tf_op jit(solution)/shard_map/psum | solution.py:12
  216.9 3.4 collective-permute-start
  220.0 11.2 copy-start.5
  234.6 3.4 copy-start.3
  238.7 192.2 %all-reduce.19.cloned.1.call-start = ((), (), s32[]{:S(2)}) async-start(), calls=%async_computation.3 | async-start | bytes 8388608 | tf_op jit(solution)/shard_map/psum | solution.py:12
  292.6 192.3 %all-reduce.21.cloned.1.call-start = ((), (), s32[]{:S(2)}) async-start(), calls=%async_computation.4 | async-start | bytes 131072 | tf_op jit(solution)/shard_map/psum | solution.py:12
  431.9 14.6 %collective-permute-start.1 = (f32[256,128]{0,1:T(8,128)S(1)}, f32[256,128]{0,1:T(8,128)S(1)}, u32[]{:S(2)}, u32[]{:S(2)}) collective-permute-start(f32[256,128]{0,1:T(8,128)S(1)} %constant_dynamic-slice_fusion.4), channel_id=1, source_target_pairs={{0,1},{1,0},{2,3},{3,2},{4,5},{5,4},{6,7},{7,6},{8,9},{9,8},{10,11... | collective-permute-start | bytes 393224 | tf_op jit(solution)/shard_map/ppermute | solution.py:16
  445.5 12.0 copy-start.9
  460.0 3.4 copy-start.2
  464.1 192.0 %all-reduce.23.cloned.1.call-start = ((), (), s32[]{:S(2)}) async-start(), calls=%async_computation.5 | async-start | bytes 8388608 | tf_op jit(solution)/shard_map/psum | solution.py:12
  517.7 182.1 %all-reduce.25.cloned.1.call-start = ((), (), s32[]{:S(2)}) async-start(), calls=%async_computation.6 | async-start | bytes 131072 | tf_op jit(solution)/shard_map/psum | solution.py:12
  657.1 3.4 collective-permute-start.2
  659.5 12.0 copy-start.7
  674.9 3.4 copy-start.4
  679.0 191.8 %all-reduce.27.cloned.1.call-start = ((), (), s32[]{:S(2)}) async-start(), calls=%async_computation.7 | async-start | bytes 8388608 | tf_op jit(solution)/shard_map/psum | solution.py:12
  732.5 181.0 %all-reduce.29.cloned.1.call-start = ((), (), s32[]{:S(2)}) async-start(), calls=%async_computation.8 | async-start | bytes 131072 | tf_op jit(solution)/shard_map/psum | solution.py:12
  871.8 3.3 collective-permute-start.3
  874.2 12.0 copy-start.10
  888.7 3.4 copy-start.1
  892.8 191.9 %all-reduce.31.cloned.1.call-start = ((), (), s32[]{:S(2)}) async-start(), calls=%async_computation.9 | async-start | bytes 8388608 | tf_op jit(solution)/shard_map/psum | solution.py:12
  946.3 182.0 %all-reduce.33.cloned.1.call-start = ((), (), s32[]{:S(2)}) async-start(), calls=%async_computation.10 | async-start | bytes 131072 | tf_op jit(solution)/shard_map/psum | solution.py:12
  1085.8 3.4 collective-permute-start.4
  1088.2 12.0 copy-start.6
  1103.6 3.4 copy-start
  1107.6 191.9 %all-reduce.35.cloned.1.call-start = ((), (), s32[]{:S(2)}) async-start(), calls=%async_computation.11 | async-start | bytes 8388608 | tf_op jit(solution)/shard_map/psum | solution.py:12
  1161.2 205.3 %all-gather.2.cloned.1.call-start = ((), (), s32[]{:S(2)}) async-start(), calls=%async_computation.12 | async-start | bytes 25165824 | tf_op jit(solution)/shard_map/all_gather | solution.py:62
  1300.5 3.3 collective-permute-start.5
  1303.8 15.2 %copy-start.8 = (f32[8192,128]{0,1:T(8,128)S(1)}, f32[8192,128]{0,1:T(8,128)}, u32[]{:S(2)}) copy-start(f32[8192,128]{0,1:T(8,128)} %all-reduce.35.cloned.1.call-done) | copy-start | bytes 12582916
  1380.6 17.8 %copy-start.11 = (s32[128]{0:T(128)S(1)}, s32[128]{0:T(128)}, u32[]{:S(2)}) copy-start(s32[128]{0:T(128)} %param.18) | copy-start | bytes 1540
Sparse Core Ops, SparseCore 0:
  17.7 26.9 all-reduce.12
  77.7 138.1 all-reduce.14
  238.8 20.9 all-reduce.16
  292.7 138.1 all-reduce.18
  464.2 20.5 all-reduce.20
  517.8 138.2 all-reduce.22
  679.1 20.5 all-reduce.24
  732.6 138.1 all-reduce.26
  892.9 20.5 all-reduce.28
  946.5 138.2 all-reduce.30
  1107.7 20.5 all-reduce.32
  1161.3 138.1 all-reduce.34
  1336.3 30.0 all-gather.1
where the time goes:
time: 1430 us; the launch traced here: 1420 us
  waiting for transfers between devices  986 us (69%)
  other arithmetic  180 us (13%)
  matrix products  129 us (9%)
  local copies, waits for them, and re-layouts  87.2 us (6%)
  starting transfers between devices  26.8 us (2%)
  between operations  14.7 us (1%)
    psum x12, waiting for transfers between devices, from_root(): return lax.psum(block, axis)  960 us
    another operation x18, other arithmetic, per_device(): cholesky_block = jnp.linalg.cholesky(diag_block)  74.3 us
    dot_general x6, matrix products, per_device(): jnp.dot(factor_halves, factor_col_rows.T, precision=lax.Precision.HIGHEST)  70.1 us
    another operation x12, other arithmetic, per_device(): jax.scipy.linalg.solve_triangular(cholesky_block, columns.T, lower=True)  62.8 us
    unnamed x27, local copies, waits for them, and re-layouts  49.5 us
    another operation x6, matrix products, per_device(): jax.scipy.linalg.solve_triangular(cholesky_block, columns.T, lower=True)  48.7 us
  transfers between devices with their start and end apart: 19, of which 19 were waited for; matrix products, arithmetic and copies ran while one was open for 1% of the time, Pallas kernels for 0%

commit v1 on v0

v1 whole, which is shorter than its diff:
```python
import functools

import jax
import jax.numpy as jnp
from jax import lax
from jax.experimental import pallas as pl
from jax.experimental.pallas import tpu as pltpu
from jax.sharding import PartitionSpec as P

B = 128
PANELS = 6
K = B * PANELS
COLS = 64
W = 256
HALF = 64
GROUP = 4
FIRST = 40
HIGHEST = lax.Precision.HIGHEST
VMEM_LIMIT = 56 * 1024 * 1024


def place(c):
    return c // 16, c // 4 % 4, c % 4


def index(y, z, x):
    return y % 4 * 16 + z % 4 * 4 + x % 4


def mirror(c):
    return (3 - c // 16) * 16 + c % 16


def send(x, pairs):
    return lax.ppermute(x, ("col", "row"), [(a[1] * 2 + a[0], b[1] * 2 + b[0]) for a, b in pairs])


def moved(c, axis, distance):
    at = list(place(c))
    at[axis] += distance
    return index(*at)


def spread(x, axis, sources, me):
    got = [
        send(x, [((0, c), (0, moved(c, axis, d))) for c in sources])
        for d in (1, -1, 2)
    ]
    return jnp.where(me == 1, got[0], jnp.where(me == 3, got[1], jnp.where(me == 2, got[2], x)))


def transpose_kernel(a_ref, t_ref):
    t_ref[...] = a_ref[...].T


def transposed_top(front):
    return pl.pallas_call(
        transpose_kernel,
        grid=(PANELS,),
        in_specs=[pl.BlockSpec((B, W), lambda i: (i, 0))],
        out_specs=pl.BlockSpec((W, B), lambda i: (0, i)),
        out_shape=jax.ShapeDtypeStruct((W, K), jnp.float32),
        name="transpose_top",
    )(front)


def dot(a, b):
    return jnp.dot(a, b, precision=HIGHEST, preferred_element_type=jnp.float32)


def solve_kernel(info_ref, blocks_ref, rhs_ref, hi_ref, lo_ref, w_ref, inv_ref, x_ref):
    w_ref[...] = jnp.zeros_like(w_ref)
    for j in range(3):
        w_ref[j * W : (j + 1) * W, j * W : (j + 1) * W] = blocks_ref[j, :W, :]
    w_ref[0:W, W : 2 * W] = blocks_ref[0, W:, :]
    w_ref[W : 2 * W, 2 * W : 3 * W] = blocks_ref[1, W:, :]
    w_ref[0:W, 2 * W : 3 * W] = blocks_ref[2, W:, :]
    for p in range(PANELS):
        w_ref[p * B : (p + 1) * B, K:] = rhs_ref[:, p * B : (p + 1) * B].T
    x_ref[...] = jnp.zeros_like(x_ref)
    sub = lax.broadcasted_iota(jnp.int32, (8, B), 0)
    lane = lax.broadcasted_iota(jnp.int32, (8, B), 1)

    @pl.loop(0, PANELS)
    def _(p):
        rows = pl.ds(pl.multiple_of(p * B, B), B)
        m = [w_ref[pl.ds(pl.multiple_of(p * B + 8 * t, 8), 8), rows] for t in range(16)]
        g = [jnp.where(lane == sub + 8 * t, 1.0, 0.0) for t in range(16)]
        for j in range(B):
            s, k = divmod(j, 8)
            pivot_row = m[s][k : k + 1, :]
            pivot_inv = g[s][k : k + 1, :]
            scale = 1.0 / m[s][k : k + 1, j : j + 1]
            for t in range(s, 16):
                if t == s and k == 7:
                    continue
                f = m[t][:, j : j + 1] * scale
                if t == s:
                    f = jnp.where(sub[:, :1] > k, f, 0.0)
                m[t] = m[t] - f * pivot_row
                g[t] = g[t] - f * pivot_inv
        for t in range(16):
            d = jnp.sum(jnp.where(lane == sub + 8 * t, m[t], 0.0), axis=1, keepdims=True)
            inv_ref[pl.ds(pl.multiple_of(p * B + 8 * t, 8), 8), :] = g[t] * (1.0 / jnp.sqrt(d))
        u = dot(inv_ref[rows, :], w_ref[rows, :])
        w_ref[rows, :] = u

        @pl.loop(p + 1, PANELS)
        def _(q):
            at = pl.ds(pl.multiple_of(q * B, B), B)
            w_ref[at, :] = w_ref[at, :] - dot(w_ref[rows, at].T, w_ref[rows, :])

    col = info_ref[1]

    @pl.when(col < 3)
    def _():
        for p in range(PANELS):
            r = lax.broadcasted_iota(jnp.int32, (B, W), 0) + p * B
            l = lax.broadcasted_iota(jnp.int32, (B, W), 1) + col * W
            w_ref[p * B : (p + 1) * B, K:] = jnp.where(r == l, 1.0, 0.0)

    @pl.loop(0, PANELS)
    def _(i):
        p = PANELS - 1 - i
        rows = pl.ds(pl.multiple_of(p * B, B), B)
        rest = w_ref[rows, K:] - dot(w_ref[rows, :K], x_ref[...])
        x_ref[rows, :] = dot(inv_ref[rows, :].T, rest)

    x = jnp.where(col < 3, -x_ref[...], x_ref[...])
    hi = x.astype(jnp.bfloat16)
    hi_ref[...] = hi
    lo_ref[...] = (x - hi.astype(jnp.float32)).astype(jnp.bfloat16)


def solve(info, blocks, rhs):
    vmem = pl.BlockSpec(memory_space=pltpu.VMEM)
    return pl.pallas_call(
        solve_kernel,
        in_specs=[pl.BlockSpec(memory_space=pltpu.SMEM), vmem, vmem],
        out_specs=[vmem, vmem],
        out_shape=[jax.ShapeDtypeStruct((K, W), jnp.bfloat16)] * 2,
        scratch_shapes=[
            pltpu.VMEM((K, K + W), jnp.float32),
            pltpu.VMEM((K, B), jnp.float32),
            pltpu.VMEM((K, W), jnp.float32),
        ],
        compiler_params=pltpu.CompilerParams(vmem_limit_bytes=VMEM_LIMIT),
        cost_estimate=pl.CostEstimate(flops=8_000_000_000, bytes_accessed=100_000_000, transcendentals=0),
        name="solve",
    )(info, blocks, rhs)


def gathered_block(r, b):
    c = r * (HALF // 2) + b // 2
    return jnp.where(b % 2 == 0, c, (3 - c // 16) * 16 + c % 16)


def block(ref, b):
    return ref.at[pl.ds(pl.multiple_of(b * B, B), B), :]


def update_kernel(leaving, info_ref, map_ref, panel_ref, front_ref, hi_ref, lo_ref, *rest):
    if leaving:
        fact_ref, send1_ref, send2_ref = rest[:3]
        rest = rest[3:]
    else:
        fact_ref, parent_ref = rest[1:3]
        rest = rest[3:]
    list_ref, panel_buf, base_buf, fact_buf, out_buf, in_sem, out_sem = rest
    r, col = info_ref[0], info_ref[1]

    def listed(b, n):
        mine = (map_ref[r * HALF + b] // HALF) == r
        take = jnp.logical_not(mine) if leaving else mine

        @pl.when(take)
        def _():
            list_ref[n] = b

        return n + take.astype(jnp.int32)

    count = lax.fori_loop(0, HALF, listed, jnp.int32(0))
    steps = (count + GROUP - 1) // GROUP

    def reads(step, j):
        slot = step % 2
        b = list_ref[step * GROUP + j]
        at = pl.ds(j * B, B)
        return (
            pltpu.make_async_copy(block(panel_ref, gathered_block(r, b)), panel_buf.at[slot, at, :], in_sem.at[slot, j, 0]),
            pltpu.make_async_copy(block(front_ref, b), base_buf.at[slot, at, :], in_sem.at[slot, j, 1]),
        )

    def each(step, act):
        for j in range(GROUP):

            @pl.when(step * GROUP + j < count)
            def _():
                act(j)

    def start_reads(step):
        def act(j):
            for copy in reads(step, j):
                copy.start()

        each(step, act)

    def wait_reads(step):
        def act(j):
            for copy in reads(step, j):
                copy.wait()

        each(step, act)

    def writes(step, do):
        slot = step % 2

        def act(j):
            n = step * GROUP + j
            b = list_ref[n]
            at = pl.ds(j * B, B)
            do(pltpu.make_async_copy(fact_buf.at[slot, at, :], block(fact_ref, b), out_sem.at[slot, j, 0]))
            source, sem = out_buf.at[slot, at, :], out_sem.at[slot, j, 1]
            if leaving:

                @pl.when(n < FIRST)
                def _():
                    do(pltpu.make_async_copy(source, block(send1_ref, n), sem))

                @pl.when(n >= FIRST)
                def _():
                    do(pltpu.make_async_copy(source, block(send2_ref, n - FIRST), sem))

            else:
                do(pltpu.make_async_copy(source, block(parent_ref, map_ref[r * HALF + b] - r * HALF), sem))

        each(step, act)

    @pl.when(steps > 0)
    def _():
        start_reads(0)

    @pl.loop(0, steps)
    def _(step):
        slot = step % 2

        @pl.when(step + 1 < steps)
        def _():
            start_reads(step + 1)

        wait_reads(step)

        @pl.when(step >= 2)
        def _():
            writes(step - 2, lambda copy: copy.wait())

        a = panel_buf[slot]
        hi = a.astype(jnp.bfloat16)
        lo = (a - hi.astype(jnp.float32)).astype(jnp.bfloat16)
        product = jnp.dot(hi, hi_ref[...], preferred_element_type=jnp.float32)
        product += jnp.dot(hi, lo_ref[...], preferred_element_type=jnp.float32)
        product += jnp.dot(lo, hi_ref[...], preferred_element_type=jnp.float32)
        lane = lax.broadcasted_iota(jnp.int32, (B, W), 1)
        first = jnp.minimum(2 * col + (lane >= B).astype(jnp.int32), PANELS)
        for j in range(GROUP):
            at = slice(j * B, (j + 1) * B)
            b = r * HALF + list_ref[jnp.minimum(step * GROUP + j, HALF - 1)]
            base = jnp.where(col < 3, 0.0, base_buf[slot, at, :])
            value = jnp.where(b >= first, base - product[at, :], 0.0)
            fact_buf[slot, at, :] = value
            out_buf[slot, at, :] = jnp.where(col < 3, 0.0, value)
        writes(step, lambda copy: copy.start())

    @pl.when(steps >= 2)
    def _():
        writes(steps - 2, lambda copy: copy.wait())

    @pl.when(steps >= 1)
    def _():
        writes(steps - 1, lambda copy: copy.wait())


def update(leaving, info, row_map, panel, front, hi, lo, factored=None):
    smem = pl.BlockSpec(memory_space=pltpu.SMEM)
    vmem = pl.BlockSpec(memory_space=pltpu.VMEM)
    hbm = pl.BlockSpec(memory_space=pl.ANY)
    whole = jax.ShapeDtypeStruct(front.shape, jnp.float32)
    if leaving:
        outs = [whole, jax.ShapeDtypeStruct((FIRST * B, W), jnp.float32), jax.ShapeDtypeStruct(((HALF - FIRST) * B, W), jnp.float32)]
        args, aliases = (), {}
    else:
        outs = [whole, whole]
        args, aliases = (factored,), {6: 0}
    return pl.pallas_call(
        functools.partial(update_kernel, leaving),
        in_specs=[smem, smem, hbm, hbm, vmem, vmem] + [hbm] * len(args),
        out_specs=[hbm] * len(outs),
        out_shape=outs,
        input_output_aliases=aliases,
        scratch_shapes=[
            pltpu.SMEM((HALF,), jnp.int32),
            pltpu.VMEM((2, GROUP * B, K), jnp.float32),
            pltpu.VMEM((2, GROUP * B, W), jnp.float32),
            pltpu.VMEM((2, GROUP * B, W), jnp.float32),
            pltpu.VMEM((2, GROUP * B, W), jnp.float32),
            pltpu.SemaphoreType.DMA((2, GROUP, 2)),
            pltpu.SemaphoreType.DMA((2, GROUP, 2)),
        ],
        compiler_params=pltpu.CompilerParams(vmem_limit_bytes=VMEM_LIMIT),
        cost_estimate=pl.CostEstimate(flops=4_800_000_000, bytes_accessed=32_000_000, transcendentals=0),
        name="update_leaving" if leaving else "update_staying",
    )(info, row_map, panel, front, hi, lo, *args)


def place_kernel(info_ref, map_ref, got1_ref, got2_ref, _, parent_ref, buf, in_sem, out_sem):
    r = info_ref[0]

    def each(do):
        def at(b, n):
            to = map_ref[(1 - r) * HALF + b] - r * HALF
            take = (to >= 0) & (to < HALF)

            @pl.when(take)
            def _():
                do(n, to)

            return n + take.astype(jnp.int32)

        lax.fori_loop(0, HALF, at, jnp.int32(0))

    def read(n, do):
        @pl.when(n < FIRST)
        def _():
            do(pltpu.make_async_copy(block(got1_ref, n), buf.at[n], in_sem.at[n]))

        @pl.when(n >= FIRST)
        def _():
            do(pltpu.make_async_copy(block(got2_ref, n - FIRST), buf.at[n], in_sem.at[n]))

    def write(n, to):
        return pltpu.make_async_copy(buf.at[n], block(parent_ref, to), out_sem.at[n])

    def pass_on(n, to):
        read(n, lambda copy: copy.wait())
        write(n, to).start()

    each(lambda n, to: read(n, lambda copy: copy.start()))
    each(pass_on)
    each(lambda n, to: write(n, to).wait())


def place_received(info, row_map, got1, got2, parent):
    smem = pl.BlockSpec(memory_space=pltpu.SMEM)
    hbm = pl.BlockSpec(memory_space=pl.ANY)
    return pl.pallas_call(
        place_kernel,
        in_specs=[smem, smem, hbm, hbm, hbm],
        out_specs=hbm,
        out_shape=jax.ShapeDtypeStruct(parent.shape, jnp.float32),
        input_output_aliases={4: 0},
        scratch_shapes=[
            pltpu.VMEM((HALF, B, W), jnp.float32),
            pltpu.SemaphoreType.DMA((HALF,)),
            pltpu.SemaphoreType.DMA((HALF,)),
        ],
        compiler_params=pltpu.CompilerParams(vmem_limit_bytes=VMEM_LIMIT),
        name="place_received",
    )(info, row_map, got1, got2, parent)


def per_device(front, row_map):
    r, c = lax.axis_index("row"), lax.axis_index("col")
    y, z, x = c // 16, c // 4 % 4, c % 4
    info = jnp.stack([r, c]).astype(jnp.int32)

    top = transposed_top(front)
    cross = send(
        top[B:],
        [((0, k), (int(place(k)[0] >= 2), mirror(k))) for k in range(COLS)],
    )
    down = send(top, [((0, k), (1, k)) for k in range(COLS)])
    mine = jnp.where(r == 0, top, down)
    piece = jnp.where((y >= 2) == (r == 1), mine[:B], cross)
    panel = lax.all_gather(piece, "col", axis=0, tiled=True)

    top, front_top, _ = lax.optimization_barrier((top, front[:K], piece))
    diag = jnp.where(c == 0, front_top[:W], jnp.where(c == 1, front_top[W : 2 * W], front_top[2 * W :]))
    off = jnp.where(c == 0, top[:, W : 2 * W], jnp.where(c == 1, top[:, 2 * W :], front_top[:W]))
    owners = [0, 1, 2]
    diag = spread(diag, 1, owners, z)
    off = spread(off, 0, owners, y)
    diag = spread(diag, 0, [k for k in range(COLS) if place(k)[0] == 0 and k % 4 < 3], y)
    off = spread(off, 1, [k for k in range(COLS) if place(k)[1] == 0 and k % 4 < 3], z)
    own = jnp.concatenate([diag, off], 0)
    near = {0: own}
    for d in (1, -1, 2):
        near[d % 4] = send(own, [((0, k), (0, moved(k, 2, d))) for k in range(COLS) if k % 4 < 3])
    blocks = []
    for j in range(3):
        d = (x - j) % 4
        blocks.append(jnp.where(d == 0, near[0], jnp.where(d == 1, near[1], jnp.where(d == 2, near[2], near[3]))))
    blocks = jnp.stack(blocks)
    blocks_down = send(blocks, [((0, k), (1, k)) for k in range(COLS)])
    blocks = jnp.where(r == 0, blocks, blocks_down)
    hi, lo = solve(info, blocks, mine)

    factored, send1, send2 = update(True, info, row_map, panel, front, hi, lo)
    swap = [((i, k), (1 - i, k)) for i in range(2) for k in range(COLS)]
    got1 = send(send1, swap)
    factored, parent = update(False, info, row_map, panel, front, hi, lo, factored)
    many = jnp.sum((row_map[:HALF] >= HALF).astype(jnp.int32)) > FIRST
    got2 = lax.cond(many, lambda v: send(v, swap), lambda v: v, send2)
    parent = place_received(info, row_map, got1, got2, parent)
    return factored, parent


def solution(mesh):
    return jax.shard_map(
        per_device,
        mesh=mesh,
        in_specs=(P("row", "col"), P()),
        out_specs=(P("row", "col"), P("row", "col")),
        check_vma=False,
    )
```

time: 1430 us -> 230 us (0.16)
  waiting for transfers between devices: 986 us -> 66.8 us
  other arithmetic: 180 us -> 4.19 us
  matrix products: 129 us -> 0 us
  Pallas kernels: 0 us -> 127 us
  local copies, waits for them, and re-layouts: 87.2 us -> 1.05 us
    psum x12 -> x0, waiting for transfers between devices: 960 us -> none  [from_root(): return lax.psum(block, axis)]
    another operation x31 -> x3, other arithmetic: 138 us -> 0.88 us  [the longest x1 0.61 us: per_device(): info = jnp.stack([r, c]).astype(jnp.int32)]
    pallas_call x0 -> x5, Pallas kernels: none -> 127 us  [the longest x1 85.4 us: solve(): pl.pallas_call(solve_kernel, in_specs=[pl.BlockSpec(memory_space=pltpu.SM...]
    dot_general x7 -> x0, matrix products: 80.4 us -> none  [the longest x6 70.1 us: per_device(): jnp.dot(factor_halves, factor_col_rows.T, precision=lax.Precision.HIGHEST)]
    ppermute x6 -> x19, waiting for transfers between devices: 5.08 us -> 66.8 us  [send(): lax.ppermute(x, ('col', 'row'), [(a[1] * 2 + a[0], b[1] * 2 + b[0]) for a...]
    unnamed x27 -> x6, local copies, waits for them, and re-layouts: 49.5 us -> 0.02 us
    another operation x6 -> x0, matrix products: 48.7 us -> none  [per_device(): jax.scipy.linalg.solve_triangular(cholesky_block, columns.T, lower=True)]
    select_n x12 -> x8, other arithmetic: 24.7 us -> 2.63 us  [the longest x1 1.34 us: per_device(): blocks = jnp.where(r == 0, blocks, blocks_down)]
  transfers between devices with their start and end apart: 19 -> 20, of which waited for: 19 -> 3; matrix products, arithmetic and copies ran while one was open for 1% -> 2% of each run, Pallas kernels for 0% -> 44%
where the time goes in v1:
time: 230 us; the launch traced here: 228 us
  Pallas kernels  127 us (55%)
  waiting for transfers between devices  66.8 us (29%)
  between operations  15.3 us (7%)
  starting transfers between devices  14.3 us (6%)
  other arithmetic  4.19 us (2%)
    pallas_call x1, Pallas kernels, solve(): pl.pallas_call(solve_kernel, in_specs=[pl.BlockSpec(memory_space=pltpu.SM...  85.4 us
    ppermute x19, waiting for transfers between devices, send(): lax.ppermute(x, ('col', 'row'), [(a[1] * 2 + a[0], b[1] * 2 + b[0]) for a...  66.8 us
    pallas_call x2, Pallas kernels, update(): pl.pallas_call(functools.partial(update_kernel, leaving), in_specs=[smem,...  31.7 us
    ppermute x19, starting transfers between devices, send(): lax.ppermute(x, ('col', 'row'), [(a[1] * 2 + a[0], b[1] * 2 + b[0]) for a...  14.3 us
    pallas_call x1, Pallas kernels, place_received(): pl.pallas_call(place_kernel, in_specs=[smem, smem, hbm, hbm, hbm], out_sp...  5.2 us
  transfers between devices with their start and end apart: 20, of which 3 were waited for; matrix products, arithmetic and copies ran while one was open for 2% of the time, Pallas kernels for 44%

profile of v1, /device:TPU:1, one launch (start us, length us, event | category | flops | bytes accessed | tf_op | source)
XLA Modules:
  0.0 228.4 jit_solution(15865866145018839033)
XLA Ops:
  7.2 4.4 %transpose_top.1 = f32[256,768]{1,0:T(8,128)} custom-call(f32[8192,256]{1,0:T(8,128)} %front_ref.3), custom_call_target="tpu_custom_call" | custom-call | tf_op jit(solution)/shard_map/transpose_top/pallas_call | solution.py:57
  11.6 1.3 collective-permute-start.1
  12.9 1.0 slice.38
  13.9 1.3 collective-permute-start.2
  15.3 1.0 collective-permute-done.1
  16.4 9.5 %collective-permute-done.2 = f32[128,768]{1,0:T(8,128)S(1)} collective-permute-done((f32[128,768]{1,0:T(8,128)S(1)}, f32[128,768]{1,0:T(8,128)S(1)}, u32[]{:S(2)}, u32[]{:S(2)}) %collective-permute-start.2) | collective-permute-done | bytes 393248 | tf_op jit(solution)/shard_map/ppermute | solution.py:35
  25.9 0.8 slice_select_fusion
  26.9 0.7 collective-permute-start.3
  27.6 0.7 collective-permute-start.4
  28.3 0.7 collective-permute-start.5
  29.0 0.7 collective-permute-start.10
  29.7 0.7 collective-permute-start.11
  30.4 0.7 collective-permute-start.9
  31.2 0.7 collective-permute-start.6
  31.9 0.7 collective-permute-start.7
  32.6 0.7 collective-permute-start.8
  33.4 0.7 collective-permute-start.12
  34.0 0.7 collective-permute-start.13
  34.7 0.7 collective-permute-start.14
  35.7 0.7 collective-permute-start.15
  36.4 0.7 collective-permute-start.16
  37.1 0.7 collective-permute-start.17
  38.2 1.3 collective-permute-start.18
  39.5 0.6 pad_add_fusion.info_ref
  40.1 56.2 %collective-permute-done.18 = f32[3,512,256]{2,1,0:T(8,128)S(1)} collective-permute-done((f32[3,512,256]{2,1,0:T(8,128)S(1)}, f32[3,512,256]{2,1,0:T(8,128)S(1)}, u32[]{:S(2)}, u32[]{:S(2)}) %collective-permute-start.18) | collective-permute-done | bytes 1572896 | tf_op jit(solution)/shard_map/ppermute | solution.py:35
  96.3 1.3 broadcast_select_fusion.blocks_ref
  97.6 85.4 %solve.1 = (bf16[768,256]{1,0:T(8,128)(2,1)}, bf16[768,256]{1,0:T(8,128)(2,1)}) custom-call(s32[2]{0:T(128)} %pad_add_fusion.info_ref, f32[3,512,256]{2,1,0:T(8,128)} %broadcast_select_fusion.blocks_ref, f32[256,768]{1,0:T(8,128)} %copy-done.1), custom_call_target="tpu_custom_call" | custom-call | flops 8000000000 | bytes 100000000 | tf_op jit(solution)/shard_map/solve/pallas_call | solution.py:137
  183.1 16.1 %update_leaving.1 = (f32[8192,256]{1,0:T(8,128)}, f32[5120,256]{1,0:T(8,128)}, f32[3072,256]{1,0:T(8,128)S(1)}) custom-call(s32[2]{0:T(128)} %pad_add_fusion.info_ref, s32[128]{0:T(128)} %map_ref.5, f32[8192,768]{1,0:T(8,128)} %all-gather.2.cloned.1.call-done.panel_ref, f32[8192,256]{1,0:T(8,128)} %front_ref.3, bf16[768,256]{1,0:T(8,128)(2,1)} %get-tuple-element.18.hi_ref, ...), custom_call_target="tpu_custom_call" | custom-call | flops 4800000000 | bytes 32000000 | tf_op jit(solution)/shard_map/update_leaving/pallas_call | solution.py:294
  199.2 0.2 collective-permute-start.19
  199.4 0.6 fusion
  200.7 15.6 %update_staying.1 = (f32[8192,256]{1,0:T(8,128)}, f32[8192,256]{1,0:T(8,128)}) custom-call(s32[2]{0:T(128)} %pad_add_fusion.info_ref, s32[128]{0:T(128)} %map_ref.5, f32[8192,768]{1,0:T(8,128)} %all-gather.2.cloned.1.call-done.panel_ref, f32[8192,256]{1,0:T(8,128)} %front_ref.3, ...), custom_call_target="tpu_custom_call", output_to_operand_aliasing={{0}: (6, {})} | custom-call | flops 4800000000 | bytes 32000000 | tf_op jit(solution)/shard_map/update_staying/pallas_call | solution.py:294
  216.3 5.2 %place_received.1 = f32[8192,256]{1,0:T(8,128)} custom-call(s32[2]{0:T(128)} %pad_add_fusion.info_ref, s32[128]{0:T(128)} %map_ref.5, f32[5120,256]{1,0:T(8,128)} %collective-permute-done.19.got1_ref, f32[3072,256]{1,0:T(8,128)S(1)} %get-tuple-element.30.got2_ref, f32[8192,256]{1,0:T(8,128)} %get-tuple-element.24._), custom_call_target="tpu_custom_call", output_to_operand_aliasing={{}: (4, {})} | custom-call | tf_op jit(solution)/shard_map/place_received/pallas_call | solution.py:355
  (37 shorter events, 0.9 us)
Async XLA Ops:
  7.2 175.9 %all-gather.2.cloned.1.call-start = ((), (), s32[]{:S(2)}) async-start(), calls=%async_computation | async-start | bytes 25559040 | tf_op jit(solution)/shard_map/all_gather | solution.py:384
  11.6 4.7 %collective-permute-start.1 = (f32[256,768]{1,0:T(8,128)}, f32[256,768]{1,0:T(8,128)S(1)}, u32[]{:S(2)}, u32[]{:S(2)}) collective-permute-start(f32[256,768]{1,0:T(8,128)} %transpose_top.1), channel_id=1, source_target_pairs={{0,1},{2,3},{4,5},{6,7},{8,9},{10,11},{12,13},{14,15},{16,17},{18,... | collective-permute-start | bytes 2359304 | tf_op jit(solution)/shard_map/ppermute | solution.py:35
  13.9 12.0 %collective-permute-start.2 = (f32[128,768]{1,0:T(8,128)S(1)}, f32[128,768]{1,0:T(8,128)S(1)}, u32[]{:S(2)}, u32[]{:S(2)}) collective-permute-start(f32[128,768]{1,0:T(8,128)S(1)} %slice.38), channel_id=1, source_target_pairs={{0,96},{2,98},{4,100},{6,102},{8,104},{10,106},{12,108},{14,110},{... | collective-permute-start | bytes 1179656 | tf_op jit(solution)/shard_map/ppermute | solution.py:35
  16.4 10.4 %copy-start.1 = (f32[256,768]{1,0:T(8,128)}, f32[256,768]{1,0:T(8,128)S(1)}, u32[]{:S(2)}) copy-start(f32[256,768]{1,0:T(8,128)S(1)} %broadcast_select_fusion.1.rhs_ref) | copy-start | bytes 2359300
  16.4 10.4 %slice-start = ((f32[8192,256]{1,0:T(8,128)}), f32[768,256]{1,0:T(8,128)S(1)}, s32[]{:S(2)}) async-start(f32[8192,256]{1,0:T(8,128)} %front_ref.3), calls=%async_computation.1 | async-start | bytes 1572864 | tf_op jit(solution)/shard_map/slice | solution.py:386
  16.4 10.4 %copy-start = (f32[256,768]{1,0:T(8,128)S(1)}, f32[256,768]{1,0:T(8,128)}, u32[]{:S(2)}) copy-start(f32[256,768]{1,0:T(8,128)} %transpose_top.1) | copy-start | bytes 2359300
  26.9 3.5 %collective-permute-start.3 = (f32[256,256]{1,0:T(8,128)S(1)}, f32[256,256]{1,0:T(8,128)S(1)}, u32[]{:S(2)}, u32[]{:S(2)}) collective-permute-start(f32[256,256]{1,0:T(8,128)S(1)} %get-tuple-element.28), channel_id=1, source_target_pairs={{0,8},{2,10},{4,12}} | collective-permute-start | bytes 786440 | tf_op jit(solution)/shard_map/ppermute | solution.py:35
  27.6 3.5 %collective-permute-start.4 = (f32[256,256]{1,0:T(8,128)S(1)}, f32[256,256]{1,0:T(8,128)S(1)}, u32[]{:S(2)}, u32[]{:S(2)}) collective-permute-start(f32[256,256]{1,0:T(8,128)S(1)} %get-tuple-element.28), channel_id=1, source_target_pairs={{0,24},{2,26},{4,28}} | collective-permute-start | bytes 786440 | tf_op jit(solution)/shard_map/ppermute | solution.py:35
  28.3 2.8 %collective-permute-start.5 = (f32[256,256]{1,0:T(8,128)S(1)}, f32[256,256]{1,0:T(8,128)S(1)}, u32[]{:S(2)}, u32[]{:S(2)}) collective-permute-start(f32[256,256]{1,0:T(8,128)S(1)} %get-tuple-element.28), channel_id=1, source_target_pairs={{0,16},{2,18},{4,20}} | collective-permute-start | bytes 786440 | tf_op jit(solution)/shard_map/ppermute | solution.py:35
  29.0 3.5 %collective-permute-start.10 = (f32[256,256]{1,0:T(8,128)S(1)}, f32[256,256]{1,0:T(8,128)S(1)}, u32[]{:S(2)}, u32[]{:S(2)}) collective-permute-start(f32[256,256]{1,0:T(8,128)S(1)} %get-tuple-element.29), channel_id=1, source_target_pairs={{0,96},{2,98},{4,100}} | collective-permute-start | bytes 786440 | tf_op jit(solution)/shard_map/ppermute | solution.py:35
  29.7 3.6 %collective-permute-start.11 = (f32[256,256]{1,0:T(8,128)S(1)}, f32[256,256]{1,0:T(8,128)S(1)}, u32[]{:S(2)}, u32[]{:S(2)}) collective-permute-start(f32[256,256]{1,0:T(8,128)S(1)} %get-tuple-element.29), channel_id=1, source_target_pairs={{0,64},{2,66},{4,68}} | collective-permute-start | bytes 786440 | tf_op jit(solution)/shard_map/ppermute | solution.py:35
  30.4 2.9 %collective-permute-start.9 = (f32[256,256]{1,0:T(8,128)S(1)}, f32[256,256]{1,0:T(8,128)S(1)}, u32[]{:S(2)}, u32[]{:S(2)}) collective-permute-start(f32[256,256]{1,0:T(8,128)S(1)} %get-tuple-element.29), channel_id=1, source_target_pairs={{0,32},{2,34},{4,36}} | collective-permute-start | bytes 786440 | tf_op jit(solution)/shard_map/ppermute | solution.py:35
  31.2 3.5 %collective-permute-start.6 = (f32[256,256]{1,0:T(8,128)S(1)}, f32[256,256]{1,0:T(8,128)S(1)}, u32[]{:S(2)}, u32[]{:S(2)}) collective-permute-start(f32[256,256]{1,0:T(8,128)S(1)} %select_select_fusion.4), channel_id=1, source_target_pairs={{0,32},{2,34},{4,36},{8,40},{10,42},{12,44},{16,48},{18,50},{20,52... | collective-permute-start | bytes 786440 | tf_op jit(solution)/shard_map/ppermute | solution.py:35
  31.9 3.5 %collective-permute-start.7 = (f32[256,256]{1,0:T(8,128)S(1)}, f32[256,256]{1,0:T(8,128)S(1)}, u32[]{:S(2)}, u32[]{:S(2)}) collective-permute-start(f32[256,256]{1,0:T(8,128)S(1)} %select_select_fusion.4), channel_id=1, source_target_pairs={{0,96},{2,98},{4,100},{8,104},{10,106},{12,108},{16,112},{18,114},... | collective-permute-start | bytes 786440 | tf_op jit(solution)/shard_map/ppermute | solution.py:35
  32.6 2.9 %collective-permute-start.8 = (f32[256,256]{1,0:T(8,128)S(1)}, f32[256,256]{1,0:T(8,128)S(1)}, u32[]{:S(2)}, u32[]{:S(2)}) collective-permute-start(f32[256,256]{1,0:T(8,128)S(1)} %select_select_fusion.4), channel_id=1, source_target_pairs={{0,64},{2,66},{4,68},{8,72},{10,74},{12,76},{16,80},{18,82},{20,84... | collective-permute-start | bytes 786440 | tf_op jit(solution)/shard_map/ppermute | solution.py:35
  33.4 2.2 collective-permute-start.12
  34.0 1.5 collective-permute-start.13
  34.7 0.8 collective-permute-start.14
  35.7 2.2 collective-permute-start.15
  36.4 1.5 collective-permute-start.16
  37.1 0.8 collective-permute-start.17
  38.2 58.1 %collective-permute-start.18 = (f32[3,512,256]{2,1,0:T(8,128)S(1)}, f32[3,512,256]{2,1,0:T(8,128)S(1)}, u32[]{:S(2)}, u32[]{:S(2)}) collective-permute-start(f32[3,512,256]{2,1,0:T(8,128)S(1)} %pad_maximum_fusion), channel_id=1, source_target_pairs={{0,1},{2,3},{4,5},{6,7},{8,9},{10,11},{12,13},{14,15},{16,17},{18,... | collective-permute-start | bytes 4718600 | tf_op jit(solution)/shard_map/ppermute | solution.py:35
  183.1 16.4 %copy-start.2 = (s32[128]{0:T(128)S(1)}, s32[128]{0:T(128)}, u32[]{:S(2)}) copy-start(s32[128]{0:T(128)} %map_ref.5) | copy-start | bytes 1540
  199.2 17.1 %collective-permute-start.19 = (f32[5120,256]{1,0:T(8,128)}, f32[5120,256]{1,0:T(8,128)}, u32[]{:S(2)}, u32[]{:S(2)}) collective-permute-start(f32[5120,256]{1,0:T(8,128)} %get-tuple-element.22), channel_id=1, source_target_pairs={{0,1},{2,3},{4,5},{6,7},{8,9},{10,11},{12,13},{14,15},{16,17},{18,... | collective-permute-start | bytes 15728648 | tf_op jit(solution)/shard_map/ppermute | solution.py:35
Sparse Core Ops, SparseCore 0:
  26.9 143.6 all-gather.1

commit v2 on v1

--- a/solution.py
+++ b/solution.py
@@ -14,6 +14,7 @@
 W = 256
 HALF = 64
 GROUP = 4
+SLOTS = 4
 FIRST = 40
 HIGHEST = lax.Precision.HIGHEST
 VMEM_LIMIT = 56 * 1024 * 1024
@@ -49,17 +50,19 @@
     return jnp.where(me == 1, got[0], jnp.where(me == 3, got[1], jnp.where(me == 2, got[2], x)))
 
 
-def transpose_kernel(a_ref, t_ref):
-    t_ref[...] = a_ref[...].T
+def transpose_kernel(a_ref, t_ref, half_ref):
+    t = a_ref[...].T
+    t_ref[...] = t
+    half_ref[...] = t[B:]
 
 
 def transposed_top(front):
     return pl.pallas_call(
         transpose_kernel,
-        grid=(PANELS,),
-        in_specs=[pl.BlockSpec((B, W), lambda i: (i, 0))],
-        out_specs=pl.BlockSpec((W, B), lambda i: (0, i)),
-        out_shape=jax.ShapeDtypeStruct((W, K), jnp.float32),
+        grid=(1,),
+        in_specs=[pl.BlockSpec((K, W), lambda i: (0, 0))],
+        out_specs=[pl.BlockSpec((W, K), lambda i: (0, 0)), pl.BlockSpec((B, K), lambda i: (0, 0))],
+        out_shape=[jax.ShapeDtypeStruct((W, K), jnp.float32), jax.ShapeDtypeStruct((B, K), jnp.float32)],
         name="transpose_top",
     )(front)
 
@@ -68,8 +71,39 @@
     return jnp.dot(a, b, precision=HIGHEST, preferred_element_type=jnp.float32)
 
 
+def eliminate(m, g, sub, inv_ref, p):
+    lane = lax.broadcasted_iota(jnp.int32, (8, B), 1)
+    for s in range(16):
+        j0 = 8 * s
+        c = [jnp.broadcast_to(m[s][:, j0 + i : j0 + i + 1], (8, B)) for i in range(8)]
+        rows, gows, coef = [], [], []
+        for k in range(8):
+            scale = 1.0 / c[k][k : k + 1, :]
+            row = m[s][k : k + 1, :] * scale
+            gow = g[s][k : k + 1, :] * scale
+            co = {i: c[i][k : k + 1, :] * scale for i in range(k + 1, 8)}
+            rows.append(row)
+            gows.append(gow)
+            coef.append(co)
+            if k < 7:
+                f = jnp.where(sub > k, c[k], 0.0)
+                for i in range(k + 1, 8):
+                    c[i] = c[i] - f * co[i]
+                m[s] = m[s] - f * row
+                g[s] = g[s] - f * gow
+        for t in range(s + 1, 16):
+            f = [jnp.broadcast_to(m[t][:, j0 + i : j0 + i + 1], (8, B)) for i in range(8)]
+            for k in range(8):
+                for i in range(k + 1, 8):
+                    f[i] = f[i] - f[k] * coef[k][i]
+                m[t] = m[t] - f[k] * rows[k]
+                g[t] = g[t] - f[k] * gows[k]
+    for t in range(16):
+        d = jnp.sum(jnp.where(lane == sub + 8 * t, m[t], 0.0), axis=1, keepdims=True)
+        inv_ref[pl.ds(pl.multiple_of(p * B + 8 * t, 8), 8), :] = g[t] * (1.0 / jnp.sqrt(d))
+
+
 def solve_kernel(info_ref, blocks_ref, rhs_ref, hi_ref, lo_ref, w_ref, inv_ref, x_ref):
-    w_ref[...] = jnp.zeros_like(w_ref)
     for j in range(3):
         w_ref[j * W : (j + 1) * W, j * W : (j + 1) * W] = blocks_ref[j, :W, :]
     w_ref[0:W, W : 2 * W] = blocks_ref[0, W:, :]
@@ -77,38 +111,25 @@
     w_ref[0:W, 2 * W : 3 * W] = blocks_ref[2, W:, :]
     for p in range(PANELS):
         w_ref[p * B : (p + 1) * B, K:] = rhs_ref[:, p * B : (p + 1) * B].T
-    x_ref[...] = jnp.zeros_like(x_ref)
     sub = lax.broadcasted_iota(jnp.int32, (8, B), 0)
     lane = lax.broadcasted_iota(jnp.int32, (8, B), 1)
 
     @pl.loop(0, PANELS)
     def _(p):
-        rows = pl.ds(pl.multiple_of(p * B, B), B)
-        m = [w_ref[pl.ds(pl.multiple_of(p * B + 8 * t, 8), 8), rows] for t in range(16)]
+        at = pl.ds(pl.multiple_of(p * B, B), B)
+        m = [w_ref[pl.ds(pl.multiple_of(p * B + 8 * t, 8), 8), at] for t in range(16)]
         g = [jnp.where(lane == sub + 8 * t, 1.0, 0.0) for t in range(16)]
-        for j in range(B):
-            s, k = divmod(j, 8)
-            pivot_row = m[s][k : k + 1, :]
-            pivot_inv = g[s][k : k + 1, :]
-            scale = 1.0 / m[s][k : k + 1, j : j + 1]
-            for t in range(s, 16):
-                if t == s and k == 7:
-                    continue
-                f = m[t][:, j : j + 1] * scale
-                if t == s:
-                    f = jnp.where(sub[:, :1] > k, f, 0.0)
-                m[t] = m[t] - f * pivot_row
-                g[t] = g[t] - f * pivot_inv
-        for t in range(16):
-            d = jnp.sum(jnp.where(lane == sub + 8 * t, m[t], 0.0), axis=1, keepdims=True)
-            inv_ref[pl.ds(pl.multiple_of(p * B + 8 * t, 8), 8), :] = g[t] * (1.0 / jnp.sqrt(d))
-        u = dot(inv_ref[rows, :], w_ref[rows, :])
-        w_ref[rows, :] = u
-
-        @pl.loop(p + 1, PANELS)
-        def _(q):
-            at = pl.ds(pl.multiple_of(q * B, B), B)
-            w_ref[at, :] = w_ref[at, :] - dot(w_ref[rows, at].T, w_ref[rows, :])
+        eliminate(m, g, sub, inv_ref, p)
+        for q in range(PANELS):
+
+            @pl.when(p == q)
+            def _():
+                rows = slice(q * B, (q + 1) * B)
+                e = (q + 1) * B
+                u = dot(inv_ref[rows, :], w_ref[rows, e:])
+                w_ref[rows, e:] = u
+                if e < K:
+                    w_ref[e:K, e:] = w_ref[e:K, e:] - dot(u[:, : K - e].T, u)
 
     col = info_ref[1]
 
@@ -118,12 +139,12 @@
             r = lax.broadcasted_iota(jnp.int32, (B, W), 0) + p * B
             l = lax.broadcasted_iota(jnp.int32, (B, W), 1) + col * W
             w_ref[p * B : (p + 1) * B, K:] = jnp.where(r == l, 1.0, 0.0)
-
-    @pl.loop(0, PANELS)
-    def _(i):
-        p = PANELS - 1 - i
-        rows = pl.ds(pl.multiple_of(p * B, B), B)
-        rest = w_ref[rows, K:] - dot(w_ref[rows, :K], x_ref[...])
+    for p in reversed(range(PANELS)):
+        rows = slice(p * B, (p + 1) * B)
+        e = (p + 1) * B
+        rest = w_ref[rows, K:]
+        if e < K:
+            rest = rest - dot(w_ref[rows, e:K], x_ref[e:, :])
         x_ref[rows, :] = dot(inv_ref[rows, :].T, rest)
 
     x = jnp.where(col < 3, -x_ref[...], x_ref[...])
@@ -183,7 +204,7 @@
     steps = (count + GROUP - 1) // GROUP
 
     def reads(step, j):
-        slot = step % 2
+        slot = step % SLOTS
         b = list_ref[step * GROUP + j]
         at = pl.ds(j * B, B)
         return (
@@ -213,7 +234,7 @@
         each(step, act)
 
     def writes(step, do):
-        slot = step % 2
+        slot = step % SLOTS
 
         def act(j):
             n = step * GROUP + j
@@ -236,23 +257,25 @@
 
         each(step, act)
 
-    @pl.when(steps > 0)
-    def _():
-        start_reads(0)
+    for ahead in range(SLOTS - 1):
+
+        @pl.when(ahead < steps)
+        def _():
+            start_reads(ahead)
 
     @pl.loop(0, steps)
     def _(step):
-        slot = step % 2
-
-        @pl.when(step + 1 < steps)
-        def _():
-            start_reads(step + 1)
+        slot = step % SLOTS
+
+        @pl.when(step + SLOTS - 1 < steps)
+        def _():
+            start_reads(step + SLOTS - 1)
 
         wait_reads(step)
 
-        @pl.when(step >= 2)
-        def _():
-            writes(step - 2, lambda copy: copy.wait())
+        @pl.when(step >= SLOTS)
+        def _():
+            writes(step - SLOTS, lambda copy: copy.wait())
 
         a = panel_buf[slot]
         hi = a.astype(jnp.bfloat16)
@@ -271,13 +294,11 @@
             out_buf[slot, at, :] = jnp.where(col < 3, 0.0, value)
         writes(step, lambda copy: copy.start())
 
-    @pl.when(steps >= 2)
-    def _():
-        writes(steps - 2, lambda copy: copy.wait())
-
-    @pl.when(steps >= 1)
-    def _():
-        writes(steps - 1, lambda copy: copy.wait())
+    for behind in range(SLOTS, 0, -1):
+
+        @pl.when(steps >= behind)
+        def _():
+            writes(steps - behind, lambda copy: copy.wait())
 
 
 def update(leaving, info, row_map, panel, front, hi, lo, factored=None):
@@ -299,12 +320,12 @@
         input_output_aliases=aliases,
         scratch_shapes=[
             pltpu.SMEM((HALF,), jnp.int32),
-            pltpu.VMEM((2, GROUP * B, K), jnp.float32),
-            pltpu.VMEM((2, GROUP * B, W), jnp.float32),
-            pltpu.VMEM((2, GROUP * B, W), jnp.float32),
-            pltpu.VMEM((2, GROUP * B, W), jnp.float32),
-            pltpu.SemaphoreType.DMA((2, GROUP, 2)),
-            pltpu.SemaphoreType.DMA((2, GROUP, 2)),
+            pltpu.VMEM((SLOTS, GROUP * B, K), jnp.float32),
+            pltpu.VMEM((SLOTS, GROUP * B, W), jnp.float32),
+            pltpu.VMEM((SLOTS, GROUP * B, W), jnp.float32),
+            pltpu.VMEM((SLOTS, GROUP * B, W), jnp.float32),
+            pltpu.SemaphoreType.DMA((SLOTS, GROUP, 2)),
+            pltpu.SemaphoreType.DMA((SLOTS, GROUP, 2)),
         ],
         compiler_params=pltpu.CompilerParams(vmem_limit_bytes=VMEM_LIMIT),
         cost_estimate=pl.CostEstimate(flops=4_800_000_000, bytes_accessed=32_000_000, transcendentals=0),
@@ -373,9 +394,9 @@
     y, z, x = c // 16, c // 4 % 4, c % 4
     info = jnp.stack([r, c]).astype(jnp.int32)
 
-    top = transposed_top(front)
+    top, top_half = transposed_top(front)
     cross = send(
-        top[B:],
+        top_half,
         [((0, k), (int(place(k)[0] >= 2), mirror(k))) for k in range(COLS)],
     )
     down = send(top, [((0, k), (1, k)) for k in range(COLS)])

time: 230 us -> 208 us (0.904)
  Pallas kernels: 127 us -> 67.1 us
  waiting for transfers between devices: 66.8 us -> 106 us
    pallas_call x1, Pallas kernels: 85.4 us -> 34.5 us  [solve(): pl.pallas_call(solve_kernel, in_specs=[pl.BlockSpec(memory_space=pltpu.SM...]
    all_gather x1, waiting for transfers between devices: 0.01 us -> 38.9 us  [per_device(): panel = lax.all_gather(piece, 'col', axis=0, tiled=True)]
    pallas_call x2, Pallas kernels: 31.7 us -> 25 us  [update(): pl.pallas_call(functools.partial(update_kernel, leaving), in_specs=[smem,...]
  transfers between devices with their start and end apart: 20 -> 20, of which waited for: 3 -> 4; matrix products, arithmetic and copies ran while one was open for 2% -> 2% of each run, Pallas kernels for 44% -> 23%
where the time goes in v2:
time: 208 us; the launch traced here: 207 us
  waiting for transfers between devices  106 us (51%)
  Pallas kernels  67.1 us (32%)
  between operations  15.3 us (7%)
  starting transfers between devices  15 us (7%)
  other arithmetic  4.23 us (2%)
    ppermute x19, waiting for transfers between devices, send(): lax.ppermute(x, ('col', 'row'), [(a[1] * 2 + a[0], b[1] * 2 + b[0]) for a...  66.9 us
    all_gather x1, waiting for transfers between devices, per_device(): panel = lax.all_gather(piece, 'col', axis=0, tiled=True)  38.9 us
    pallas_call x1, Pallas kernels, solve(): pl.pallas_call(solve_kernel, in_specs=[pl.BlockSpec(memory_space=pltpu.SM...  34.5 us
    pallas_call x2, Pallas kernels, update(): pl.pallas_call(functools.partial(update_kernel, leaving), in_specs=[smem,...  25 us
    ppermute x19, starting transfers between devices, send(): lax.ppermute(x, ('col', 'row'), [(a[1] * 2 + a[0], b[1] * 2 + b[0]) for a...  15 us
    pallas_call x1, Pallas kernels, place_received(): pl.pallas_call(place_kernel, in_specs=[smem, smem, hbm, hbm, hbm], out_sp...  5.17 us
  transfers between devices with their start and end apart: 20, of which 4 were waited for; matrix products, arithmetic and copies ran while one was open for 2% of the time, Pallas kernels for 23%

profile of v2, /device:TPU:1, one launch (start us, length us, event | category | flops | bytes accessed | tf_op | source)
XLA Modules:
  0.0 207.4 jit_solution(6384347758865998885)
XLA Ops:
  7.2 2.4 %transpose_top.1 = (f32[256,768]{1,0:T(8,128)}, f32[128,768]{1,0:T(8,128)}) custom-call(f32[8192,256]{1,0:T(8,128)} %front_ref.3), custom_call_target="tpu_custom_call" | custom-call | tf_op jit(solution)/shard_map/transpose_top/pallas_call | solution.py:60
  9.6 1.3 collective-permute-start.1
  10.9 1.3 collective-permute-start.2
  12.2 2.1 collective-permute-done.1
  14.4 8.7 %collective-permute-done.2 = f32[128,768]{1,0:T(8,128)S(1)} collective-permute-done((f32[128,768]{1,0:T(8,128)}, f32[128,768]{1,0:T(8,128)S(1)}, u32[]{:S(2)}, u32[]{:S(2)}) %collective-permute-start.2) | collective-permute-done | bytes 393248 | tf_op jit(solution)/shard_map/ppermute | solution.py:36
  23.1 0.9 slice_select_fusion
  24.1 0.7 collective-permute-start.3
  24.8 0.7 collective-permute-start.4
  25.5 0.7 collective-permute-start.5
  26.2 0.7 collective-permute-start.10
  26.9 0.7 collective-permute-start.11
  27.6 0.7 collective-permute-start.9
  28.4 0.7 collective-permute-start.6
  29.1 0.7 collective-permute-start.7
  29.8 0.7 collective-permute-start.8
  30.5 0.7 collective-permute-start.12
  31.2 0.7 collective-permute-start.13
  31.9 0.7 collective-permute-start.14
  32.9 0.7 collective-permute-start.15
  33.6 0.7 collective-permute-start.16
  34.3 0.7 collective-permute-start.17
  35.4 1.5 collective-permute-start.18
  36.8 0.6 pad_add_fusion.info_ref
  37.5 56.1 %collective-permute-done.18 = f32[3,512,256]{2,1,0:T(8,128)S(1)} collective-permute-done((f32[3,512,256]{2,1,0:T(8,128)S(1)}, f32[3,512,256]{2,1,0:T(8,128)S(1)}, u32[]{:S(2)}, u32[]{:S(2)}) %collective-permute-start.18) | collective-permute-done | bytes 1572896 | tf_op jit(solution)/shard_map/ppermute | solution.py:36
  93.6 1.3 broadcast_select_fusion.blocks_ref
  94.9 34.5 %solve.1 = (bf16[768,256]{1,0:T(8,128)(2,1)}, bf16[768,256]{1,0:T(8,128)(2,1)}) custom-call(s32[2]{0:T(128)} %pad_add_fusion.info_ref, f32[3,512,256]{2,1,0:T(8,128)} %broadcast_select_fusion.blocks_ref, f32[256,768]{1,0:T(8,128)} %copy-done.1), custom_call_target="tpu_custom_call" | custom-call | flops 8000000000 | bytes 100000000 | tf_op jit(solution)/shard_map/solve/pallas_call | solution.py:158
  129.4 38.9 %all-gather.2.cloned.1.call-done.panel_ref = f32[8192,768]{1,0:T(8,128)} async-done(((f32[128,768]{1,0:T(8,128)}), f32[8192,768]{1,0:T(8,128)}) %all-gather.2.cloned.1.call-update) | async-done | bytes 25165840 | tf_op jit(solution)/shard_map/all_gather | solution.py:405
  168.3 12.5 %update_leaving.1 = (f32[8192,256]{1,0:T(8,128)}, f32[5120,256]{1,0:T(8,128)}, f32[3072,256]{1,0:T(8,128)S(1)}) custom-call(s32[2]{0:T(128)} %pad_add_fusion.info_ref, s32[128]{0:T(128)} %map_ref.5, f32[8192,768]{1,0:T(8,128)} %all-gather.2.cloned.1.call-done.panel_ref, f32[8192,256]{1,0:T(8,128)} %front_ref.3, bf16[768,256]{1,0:T(8,128)(2,1)} %get-tuple-element.22.hi_ref, ...), custom_call_target="tpu_custom_call" | custom-call | flops 4800000000 | bytes 32000000 | tf_op jit(solution)/shard_map/update_leaving/pallas_call | solution.py:315
  180.8 0.8 collective-permute-start.19
  181.5 0.6 fusion
  182.8 12.5 %update_staying.1 = (f32[8192,256]{1,0:T(8,128)}, f32[8192,256]{1,0:T(8,128)}) custom-call(s32[2]{0:T(128)} %pad_add_fusion.info_ref, s32[128]{0:T(128)} %map_ref.5, f32[8192,768]{1,0:T(8,128)} %all-gather.2.cloned.1.call-done.panel_ref, f32[8192,256]{1,0:T(8,128)} %front_ref.3, ...), custom_call_target="tpu_custom_call", output_to_operand_aliasing={{0}: (6, {})} | custom-call | flops 4800000000 | bytes 32000000 | tf_op jit(solution)/shard_map/update_staying/pallas_call | solution.py:315
  195.4 5.2 %place_received.1 = f32[8192,256]{1,0:T(8,128)} custom-call(s32[2]{0:T(128)} %pad_add_fusion.info_ref, s32[128]{0:T(128)} %map_ref.5, f32[5120,256]{1,0:T(8,128)} %collective-permute-done.19.got1_ref, f32[3072,256]{1,0:T(8,128)S(1)} %get-tuple-element.34.got2_ref, f32[8192,256]{1,0:T(8,128)} %get-tuple-element.28._), custom_call_target="tpu_custom_call", output_to_operand_aliasing={{}: (4, {})} | custom-call | tf_op jit(solution)/shard_map/place_received/pallas_call | solution.py:376
  (36 shorter events, 0.9 us)
Async XLA Ops:
  7.2 161.1 %all-gather.2.cloned.1.call-start = ((), (), s32[]{:S(2)}) async-start(), calls=%async_computation | async-start | bytes 25559040 | tf_op jit(solution)/shard_map/all_gather | solution.py:405
  9.6 4.7 %collective-permute-start.1 = (f32[256,768]{1,0:T(8,128)}, f32[256,768]{1,0:T(8,128)S(1)}, u32[]{:S(2)}, u32[]{:S(2)}) collective-permute-start(f32[256,768]{1,0:T(8,128)} %get-tuple-element.21), channel_id=1, source_target_pairs={{0,1},{2,3},{4,5},{6,7},{8,9},{10,11},{12,13},{14,15},{16,17},{18,... | collective-permute-start | bytes 2359304 | tf_op jit(solution)/shard_map/ppermute | solution.py:36
  10.9 12.2 %collective-permute-start.2 = (f32[128,768]{1,0:T(8,128)}, f32[128,768]{1,0:T(8,128)S(1)}, u32[]{:S(2)}, u32[]{:S(2)}) collective-permute-start(f32[128,768]{1,0:T(8,128)} %get-tuple-element.19), channel_id=1, source_target_pairs={{0,96},{2,98},{4,100},{6,102},{8,104},{10,106},{12,108},{14,110},{... | collective-permute-start | bytes 1179656 | tf_op jit(solution)/shard_map/ppermute | solution.py:36
  14.4 9.6 %copy-start.1 = (f32[256,768]{1,0:T(8,128)}, f32[256,768]{1,0:T(8,128)S(1)}, u32[]{:S(2)}) copy-start(f32[256,768]{1,0:T(8,128)S(1)} %broadcast_select_fusion.1.rhs_ref) | copy-start | bytes 2359300
  14.4 9.6 %slice-start = ((f32[8192,256]{1,0:T(8,128)}), f32[768,256]{1,0:T(8,128)S(1)}, s32[]{:S(2)}) async-start(f32[8192,256]{1,0:T(8,128)} %front_ref.3), calls=%async_computation.1 | async-start | bytes 1572864 | tf_op jit(solution)/shard_map/slice | solution.py:407
  14.4 9.6 %copy-start = (f32[256,768]{1,0:T(8,128)S(1)}, f32[256,768]{1,0:T(8,128)}, u32[]{:S(2)}) copy-start(f32[256,768]{1,0:T(8,128)} %get-tuple-element.21) | copy-start | bytes 2359300
  24.1 3.5 %collective-permute-start.3 = (f32[256,256]{1,0:T(8,128)S(1)}, f32[256,256]{1,0:T(8,128)S(1)}, u32[]{:S(2)}, u32[]{:S(2)}) collective-permute-start(f32[256,256]{1,0:T(8,128)S(1)} %get-tuple-element.32), channel_id=1, source_target_pairs={{0,8},{2,10},{4,12}} | collective-permute-start | bytes 786440 | tf_op jit(solution)/shard_map/ppermute | solution.py:36
  24.8 3.5 %collective-permute-start.4 = (f32[256,256]{1,0:T(8,128)S(1)}, f32[256,256]{1,0:T(8,128)S(1)}, u32[]{:S(2)}, u32[]{:S(2)}) collective-permute-start(f32[256,256]{1,0:T(8,128)S(1)} %get-tuple-element.32), channel_id=1, source_target_pairs={{0,24},{2,26},{4,28}} | collective-permute-start | bytes 786440 | tf_op jit(solution)/shard_map/ppermute | solution.py:36
  25.5 2.8 %collective-permute-start.5 = (f32[256,256]{1,0:T(8,128)S(1)}, f32[256,256]{1,0:T(8,128)S(1)}, u32[]{:S(2)}, u32[]{:S(2)}) collective-permute-start(f32[256,256]{1,0:T(8,128)S(1)} %get-tuple-element.32), channel_id=1, source_target_pairs={{0,16},{2,18},{4,20}} | collective-permute-start | bytes 786440 | tf_op jit(solution)/shard_map/ppermute | solution.py:36
  26.2 3.5 %collective-permute-start.10 = (f32[256,256]{1,0:T(8,128)S(1)}, f32[256,256]{1,0:T(8,128)S(1)}, u32[]{:S(2)}, u32[]{:S(2)}) collective-permute-start(f32[256,256]{1,0:T(8,128)S(1)} %get-tuple-element.33), channel_id=1, source_target_pairs={{0,96},{2,98},{4,100}} | collective-permute-start | bytes 786440 | tf_op jit(solution)/shard_map/ppermute | solution.py:36
  26.9 3.6 %collective-permute-start.11 = (f32[256,256]{1,0:T(8,128)S(1)}, f32[256,256]{1,0:T(8,128)S(1)}, u32[]{:S(2)}, u32[]{:S(2)}) collective-permute-start(f32[256,256]{1,0:T(8,128)S(1)} %get-tuple-element.33), channel_id=1, source_target_pairs={{0,64},{2,66},{4,68}} | collective-permute-start | bytes 786440 | tf_op jit(solution)/shard_map/ppermute | solution.py:36
  27.6 2.9 %collective-permute-start.9 = (f32[256,256]{1,0:T(8,128)S(1)}, f32[256,256]{1,0:T(8,128)S(1)}, u32[]{:S(2)}, u32[]{:S(2)}) collective-permute-start(f32[256,256]{1,0:T(8,128)S(1)} %get-tuple-element.33), channel_id=1, source_target_pairs={{0,32},{2,34},{4,36}} | collective-permute-start | bytes 786440 | tf_op jit(solution)/shard_map/ppermute | solution.py:36
  28.4 3.5 %collective-permute-start.6 = (f32[256,256]{1,0:T(8,128)S(1)}, f32[256,256]{1,0:T(8,128)S(1)}, u32[]{:S(2)}, u32[]{:S(2)}) collective-permute-start(f32[256,256]{1,0:T(8,128)S(1)} %select_select_fusion.4), channel_id=1, source_target_pairs={{0,32},{2,34},{4,36},{8,40},{10,42},{12,44},{16,48},{18,50},{20,52... | collective-permute-start | bytes 786440 | tf_op jit(solution)/shard_map/ppermute | solution.py:36
  29.1 3.5 %collective-permute-start.7 = (f32[256,256]{1,0:T(8,128)S(1)}, f32[256,256]{1,0:T(8,128)S(1)}, u32[]{:S(2)}, u32[]{:S(2)}) collective-permute-start(f32[256,256]{1,0:T(8,128)S(1)} %select_select_fusion.4), channel_id=1, source_target_pairs={{0,96},{2,98},{4,100},{8,104},{10,106},{12,108},{16,112},{18,114},... | collective-permute-start | bytes 786440 | tf_op jit(solution)/shard_map/ppermute | solution.py:36
  29.8 2.9 %collective-permute-start.8 = (f32[256,256]{1,0:T(8,128)S(1)}, f32[256,256]{1,0:T(8,128)S(1)}, u32[]{:S(2)}, u32[]{:S(2)}) collective-permute-start(f32[256,256]{1,0:T(8,128)S(1)} %select_select_fusion.4), channel_id=1, source_target_pairs={{0,64},{2,66},{4,68},{8,72},{10,74},{12,76},{16,80},{18,82},{20,84... | collective-permute-start | bytes 786440 | tf_op jit(solution)/shard_map/ppermute | solution.py:36
  30.5 2.2 %collective-permute-start.12 = (f32[256,256]{1,0:T(8,128)S(1)}, f32[256,256]{1,0:T(8,128)S(1)}, u32[]{:S(2)}, u32[]{:S(2)}) collective-permute-start(f32[256,256]{1,0:T(8,128)S(1)} %select_select_fusion.1), channel_id=1, source_target_pairs={{0,8},{2,10},{4,12},{32,40},{34,42},{36,44},{64,72},{66,74},{68,76... | collective-permute-start | bytes 786440 | tf_op jit(solution)/shard_map/ppermute | solution.py:36
  31.2 1.5 collective-permute-start.13
  31.9 0.8 collective-permute-start.14
  32.9 2.2 %collective-permute-start.15 = (f32[512,256]{1,0:T(8,128)S(1)}, f32[512,256]{1,0:T(8,128)S(1)}, u32[]{:S(2)}, u32[]{:S(2)}) collective-permute-start(f32[512,256]{1,0:T(8,128)S(1)} %pad_maximum_fusion.1), channel_id=1, source_target_pairs={{0,2},{2,4},{4,6},{8,10},{10,12},{12,14},{16,18},{18,20},{20,22},{... | collective-permute-start | bytes 1572872 | tf_op jit(solution)/shard_map/ppermute | solution.py:36
  33.6 1.5 collective-permute-start.16
  34.3 0.8 collective-permute-start.17
  35.4 58.2 %collective-permute-start.18 = (f32[3,512,256]{2,1,0:T(8,128)S(1)}, f32[3,512,256]{2,1,0:T(8,128)S(1)}, u32[]{:S(2)}, u32[]{:S(2)}) collective-permute-start(f32[3,512,256]{2,1,0:T(8,128)S(1)} %pad_maximum_fusion), channel_id=1, source_target_pairs={{0,1},{2,3},{4,5},{6,7},{8,9},{10,11},{12,13},{14,15},{16,17},{18,... | collective-permute-start | bytes 4718600 | tf_op jit(solution)/shard_map/ppermute | solution.py:36
  168.3 13.3 %copy-start.2 = (s32[128]{0:T(128)S(1)}, s32[128]{0:T(128)}, u32[]{:S(2)}) copy-start(s32[128]{0:T(128)} %map_ref.5) | copy-start | bytes 1540
  180.8 14.6 %collective-permute-start.19 = (f32[5120,256]{1,0:T(8,128)}, f32[5120,256]{1,0:T(8,128)}, u32[]{:S(2)}, u32[]{:S(2)}) collective-permute-start(f32[5120,256]{1,0:T(8,128)} %get-tuple-element.26), channel_id=1, source_target_pairs={{0,1},{2,3},{4,5},{6,7},{8,9},{10,11},{12,13},{14,15},{16,17},{18,... | collective-permute-start | bytes 15728648 | tf_op jit(solution)/shard_map/ppermute | solution.py:36
Sparse Core Ops, SparseCore 0:
  24.1 144.1 all-gather.1

commit v3 on v2

--- a/solution.py
+++ b/solution.py
@@ -43,11 +43,10 @@
 
 
 def spread(x, axis, sources, me):
-    got = [
-        send(x, [((0, c), (0, moved(c, axis, d))) for c in sources])
-        for d in (1, -1, 2)
-    ]
-    return jnp.where(me == 1, got[0], jnp.where(me == 3, got[1], jnp.where(me == 2, got[2], x)))
+    up = send(x, [((0, c), (0, moved(c, axis, 1))) for c in sources])
+    down = send(x, [((0, c), (0, moved(c, axis, -1))) for c in sources])
+    far = send(up, [((0, moved(c, axis, 1)), (0, moved(c, axis, 2))) for c in sources])
+    return jnp.where(me == 1, up, jnp.where(me == 3, down, jnp.where(me == 2, far, x)))
 
 
 def transpose_kernel(a_ref, t_ref, half_ref):
@@ -103,7 +102,29 @@
         inv_ref[pl.ds(pl.multiple_of(p * B + 8 * t, 8), 8), :] = g[t] * (1.0 / jnp.sqrt(d))
 
 
-def solve_kernel(info_ref, blocks_ref, rhs_ref, hi_ref, lo_ref, w_ref, inv_ref, x_ref):
+def plan(info_ref, map_ref, plan_ref):
+    r = info_ref[0]
+
+    def at(b, counts):
+        leaving, staying, coming = counts
+        leaves = (map_ref[r * HALF + b] // HALF != r).astype(jnp.int32)
+        to = map_ref[(1 - r) * HALF + b]
+        comes = (to // HALF == r).astype(jnp.int32)
+        plan_ref[jnp.where(leaves == 1, leaving, HALF + staying)] = b
+
+        @pl.when(comes == 1)
+        def _():
+            plan_ref[2 * HALF + coming] = to - r * HALF
+
+        return leaving + leaves, staying + 1 - leaves, coming + comes
+
+    counts = lax.fori_loop(0, HALF, at, (jnp.int32(0),) * 3)
+    for i, count in enumerate(counts):
+        plan_ref[3 * HALF + i] = count
+
+
+def solve_kernel(info_ref, map_ref, blocks_ref, rhs_ref, hi_ref, lo_ref, plan_ref, w_ref, inv_ref, x_ref):
+    plan(info_ref, map_ref, plan_ref)
     for j in range(3):
         w_ref[j * W : (j + 1) * W, j * W : (j + 1) * W] = blocks_ref[j, :W, :]
     w_ref[0:W, W : 2 * W] = blocks_ref[0, W:, :]
@@ -153,13 +174,14 @@
     lo_ref[...] = (x - hi.astype(jnp.float32)).astype(jnp.bfloat16)
 
 
-def solve(info, blocks, rhs):
+def solve(info, row_map, blocks, rhs):
     vmem = pl.BlockSpec(memory_space=pltpu.VMEM)
+    smem = pl.BlockSpec(memory_space=pltpu.SMEM)
     return pl.pallas_call(
         solve_kernel,
-        in_specs=[pl.BlockSpec(memory_space=pltpu.SMEM), vmem, vmem],
-        out_specs=[vmem, vmem],
-        out_shape=[jax.ShapeDtypeStruct((K, W), jnp.bfloat16)] * 2,
+        in_specs=[smem, smem, vmem, vmem],
+        out_specs=[vmem, vmem, smem],
+        out_shape=[jax.ShapeDtypeStruct((K, W), jnp.bfloat16)] * 2 + [jax.ShapeDtypeStruct((4 * HALF,), jnp.int32)],
         scratch_shapes=[
             pltpu.VMEM((K, K + W), jnp.float32),
             pltpu.VMEM((K, B), jnp.float32),
@@ -168,7 +190,7 @@
         compiler_params=pltpu.CompilerParams(vmem_limit_bytes=VMEM_LIMIT),
         cost_estimate=pl.CostEstimate(flops=8_000_000_000, bytes_accessed=100_000_000, transcendentals=0),
         name="solve",
-    )(info, blocks, rhs)
+    )(info, row_map, blocks, rhs)
 
 
 def gathered_block(r, b):
@@ -180,32 +202,23 @@
     return ref.at[pl.ds(pl.multiple_of(b * B, B), B), :]
 
 
-def update_kernel(leaving, info_ref, map_ref, panel_ref, front_ref, hi_ref, lo_ref, *rest):
+def update_kernel(leaving, info_ref, map_ref, plan_ref, panel_ref, front_ref, hi_ref, lo_ref, *rest):
     if leaving:
         fact_ref, send1_ref, send2_ref = rest[:3]
         rest = rest[3:]
     else:
         fact_ref, parent_ref = rest[1:3]
         rest = rest[3:]
-    list_ref, panel_buf, base_buf, fact_buf, out_buf, in_sem, out_sem = rest
+    panel_buf, base_buf, fact_buf, out_buf, in_sem, out_sem = rest
     r, col = info_ref[0], info_ref[1]
 
-    def listed(b, n):
-        mine = (map_ref[r * HALF + b] // HALF) == r
-        take = jnp.logical_not(mine) if leaving else mine
-
-        @pl.when(take)
-        def _():
-            list_ref[n] = b
-
-        return n + take.astype(jnp.int32)
-
-    count = lax.fori_loop(0, HALF, listed, jnp.int32(0))
+    first_entry = 0 if leaving else HALF
+    count = plan_ref[3 * HALF + (0 if leaving else 1)]
     steps = (count + GROUP - 1) // GROUP
 
     def reads(step, j):
         slot = step % SLOTS
-        b = list_ref[step * GROUP + j]
+        b = plan_ref[first_entry + step * GROUP + j]
         at = pl.ds(j * B, B)
         return (
             pltpu.make_async_copy(block(panel_ref, gathered_block(r, b)), panel_buf.at[slot, at, :], in_sem.at[slot, j, 0]),
@@ -238,7 +251,7 @@
 
         def act(j):
             n = step * GROUP + j
-            b = list_ref[n]
+            b = plan_ref[first_entry + n]
             at = pl.ds(j * B, B)
             do(pltpu.make_async_copy(fact_buf.at[slot, at, :], block(fact_ref, b), out_sem.at[slot, j, 0]))
             source, sem = out_buf.at[slot, at, :], out_sem.at[slot, j, 1]
@@ -287,7 +300,7 @@
         first = jnp.minimum(2 * col + (lane >= B).astype(jnp.int32), PANELS)
         for j in range(GROUP):
             at = slice(j * B, (j + 1) * B)
-            b = r * HALF + list_ref[jnp.minimum(step * GROUP + j, HALF - 1)]
+            b = r * HALF + plan_ref[first_entry + jnp.minimum(step * GROUP + j, count - 1)]
             base = jnp.where(col < 3, 0.0, base_buf[slot, at, :])
             value = jnp.where(b >= first, base - product[at, :], 0.0)
             fact_buf[slot, at, :] = value
@@ -301,7 +314,7 @@
             writes(steps - behind, lambda copy: copy.wait())
 
 
-def update(leaving, info, row_map, panel, front, hi, lo, factored=None):
+def update(leaving, info, row_map, lists, panel, front, hi, lo, factored=None):
     smem = pl.BlockSpec(memory_space=pltpu.SMEM)
     vmem = pl.BlockSpec(memory_space=pltpu.VMEM)
     hbm = pl.BlockSpec(memory_space=pl.ANY)
@@ -311,15 +324,14 @@
         args, aliases = (), {}
     else:
         outs = [whole, whole]
-        args, aliases = (factored,), {6: 0}
+        args, aliases = (factored,), {7: 0}
     return pl.pallas_call(
         functools.partial(update_kernel, leaving),
-        in_specs=[smem, smem, hbm, hbm, vmem, vmem] + [hbm] * len(args),
+        in_specs=[smem, smem, smem, hbm, hbm, vmem, vmem] + [hbm] * len(args),
         out_specs=[hbm] * len(outs),
         out_shape=outs,
         input_output_aliases=aliases,
         scratch_shapes=[
-            pltpu.SMEM((HALF,), jnp.int32),
             pltpu.VMEM((SLOTS, GROUP * B, K), jnp.float32),
             pltpu.VMEM((SLOTS, GROUP * B, W), jnp.float32),
             pltpu.VMEM((SLOTS, GROUP * B, W), jnp.float32),
@@ -330,55 +342,46 @@
         compiler_params=pltpu.CompilerParams(vmem_limit_bytes=VMEM_LIMIT),
         cost_estimate=pl.CostEstimate(flops=4_800_000_000, bytes_accessed=32_000_000, transcendentals=0),
         name="update_leaving" if leaving else "update_staying",
-    )(info, row_map, panel, front, hi, lo, *args)
-
-
-def place_kernel(info_ref, map_ref, got1_ref, got2_ref, _, parent_ref, buf, in_sem, out_sem):
-    r = info_ref[0]
-
-    def each(do):
-        def at(b, n):
-            to = map_ref[(1 - r) * HALF + b] - r * HALF
-            take = (to >= 0) & (to < HALF)
-
-            @pl.when(take)
-            def _():
-                do(n, to)
-
-            return n + take.astype(jnp.int32)
-
-        lax.fori_loop(0, HALF, at, jnp.int32(0))
-
-    def read(n, do):
-        @pl.when(n < FIRST)
-        def _():
-            do(pltpu.make_async_copy(block(got1_ref, n), buf.at[n], in_sem.at[n]))
-
-        @pl.when(n >= FIRST)
-        def _():
-            do(pltpu.make_async_copy(block(got2_ref, n - FIRST), buf.at[n], in_sem.at[n]))
-
-    def write(n, to):
-        return pltpu.make_async_copy(buf.at[n], block(parent_ref, to), out_sem.at[n])
-
-    def pass_on(n, to):
-        read(n, lambda copy: copy.wait())
-        write(n, to).start()
-
-    each(lambda n, to: read(n, lambda copy: copy.start()))
-    each(pass_on)
-    each(lambda n, to: write(n, to).wait())
-
-
-def place_received(info, row_map, got1, got2, parent):
+    )(info, row_map, lists, panel, front, hi, lo, *args)
+
+
+def place_kernel(plan_ref, got1_ref, got2_ref, _, parent_ref, buf, in_sem, out_sem):
+    def read1(n):
+        return pltpu.make_async_copy(block(got1_ref, n), buf.at[n], in_sem.at[n])
+
+    def read2(n):
+        return pltpu.make_async_copy(block(got2_ref, n - FIRST), buf.at[n], in_sem.at[n])
+
+    def write(n):
+        return pltpu.make_async_copy(buf.at[n], block(parent_ref, plan_ref[2 * HALF + n]), out_sem.at[n])
+
+    def each(first, last, act):
+        @pl.loop(first, last)
+        def _(n):
+            act(n)
+
+    def pass_on(copy, n):
+        copy.wait()
+        write(n).start()
+
+    count = plan_ref[3 * HALF + 2]
+    split = jnp.minimum(count, FIRST)
+    each(0, split, lambda n: read1(n).start())
+    each(split, count, lambda n: read2(n).start())
+    each(0, split, lambda n: pass_on(read1(n), n))
+    each(split, count, lambda n: pass_on(read2(n), n))
+    each(0, count, lambda n: write(n).wait())
+
+
+def place_received(lists, got1, got2, parent):
     smem = pl.BlockSpec(memory_space=pltpu.SMEM)
     hbm = pl.BlockSpec(memory_space=pl.ANY)
     return pl.pallas_call(
         place_kernel,
-        in_specs=[smem, smem, hbm, hbm, hbm],
+        in_specs=[smem, hbm, hbm, hbm],
         out_specs=hbm,
         out_shape=jax.ShapeDtypeStruct(parent.shape, jnp.float32),
-        input_output_aliases={4: 0},
+        input_output_aliases={3: 0},
         scratch_shapes=[
             pltpu.VMEM((HALF, B, W), jnp.float32),
             pltpu.SemaphoreType.DMA((HALF,)),
@@ -386,7 +389,7 @@
         ],
         compiler_params=pltpu.CompilerParams(vmem_limit_bytes=VMEM_LIMIT),
         name="place_received",
-    )(info, row_map, got1, got2, parent)
+    )(lists, got1, got2, parent)
 
 
 def per_device(front, row_map):
@@ -414,8 +417,13 @@
     off = spread(off, 1, [k for k in range(COLS) if place(k)[1] == 0 and k % 4 < 3], z)
     own = jnp.concatenate([diag, off], 0)
     near = {0: own}
-    for d in (1, -1, 2):
+    for d in (1, -1):
         near[d % 4] = send(own, [((0, k), (0, moved(k, 2, d))) for k in range(COLS) if k % 4 < 3])
+    halves = [
+        send(near[1][:W], [((0, moved(k, 2, 1)), (0, moved(k, 2, 2))) for k in range(COLS) if k % 4 < 3]),
+        send(near[3][W:], [((0, moved(k, 2, -1)), (0, moved(k, 2, -2))) for k in range(COLS) if k % 4 < 3]),
+    ]
+    near[2] = jnp.concatenate(halves, 0)
     blocks = []
     for j in range(3):
         d = (x - j) % 4
@@ -423,15 +431,15 @@
     blocks = jnp.stack(blocks)
     blocks_down = send(blocks, [((0, k), (1, k)) for k in range(COLS)])
     blocks = jnp.where(r == 0, blocks, blocks_down)
-    hi, lo = solve(info, blocks, mine)
-
-    factored, send1, send2 = update(True, info, row_map, panel, front, hi, lo)
+    hi, lo, lists = solve(info, row_map, blocks, mine)
+
+    factored, send1, send2 = update(True, info, row_map, lists, panel, front, hi, lo)
     swap = [((i, k), (1 - i, k)) for i in range(2) for k in range(COLS)]
     got1 = send(send1, swap)
-    factored, parent = update(False, info, row_map, panel, front, hi, lo, factored)
+    factored, parent = update(False, info, row_map, lists, panel, front, hi, lo, factored)
     many = jnp.sum((row_map[:HALF] >= HALF).astype(jnp.int32)) > FIRST
     got2 = lax.cond(many, lambda v: send(v, swap), lambda v: v, send2)
-    parent = place_received(info, row_map, got1, got2, parent)
+    parent = place_received(lists, got1, got2, parent)
     return factored, parent
 
 

time: 208 us -> 202 us (0.971)
  waiting for transfers between devices: 106 us -> 98.4 us
    all_gather x1, waiting for transfers between devices: 38.9 us -> 34.5 us  [per_device(): panel = lax.all_gather(piece, 'col', axis=0, tiled=True)]
    ppermute x19 -> x20, waiting for transfers between devices: 66.9 us -> 63.9 us  [send(): lax.ppermute(x, ('col', 'row'), [(a[1] * 2 + a[0], b[1] * 2 + b[0]) for a...]
    pallas_call x2, Pallas kernels: 39.6 us -> 42.3 us  [the longest x1 36.5 us: solve(): pl.pallas_call(solve_kernel, in_specs=[smem, smem, vmem, vmem], out_specs...]
    pallas_call x2, Pallas kernels: 25 us -> 22.8 us  [update(): pl.pallas_call(functools.partial(update_kernel, leaving), in_specs=[smem,...]
    ppermute x19 -> x20, starting transfers between devices: 15 us -> 15.7 us  [send(): lax.ppermute(x, ('col', 'row'), [(a[1] * 2 + a[0], b[1] * 2 + b[0]) for a...]
  transfers between devices with their start and end apart: 20 -> 21, of which waited for: 4 -> 4; matrix products, arithmetic and copies ran while one was open for 2% -> 2% of each run, Pallas kernels for 23% -> 24%
where the time goes in v3:
time: 202 us; the launch traced here: 201 us
  waiting for transfers between devices  98.4 us (49%)
  Pallas kernels  67.6 us (33%)
  starting transfers between devices  15.7 us (8%)
  between operations  15.3 us (8%)
  other arithmetic  4.24 us (2%)
    ppermute x20, waiting for transfers between devices, send(): lax.ppermute(x, ('col', 'row'), [(a[1] * 2 + a[0], b[1] * 2 + b[0]) for a...  63.9 us
    pallas_call x1, Pallas kernels, solve(): pl.pallas_call(solve_kernel, in_specs=[smem, smem, vmem, vmem], out_specs...  36.5 us
    all_gather x1, waiting for transfers between devices, per_device(): panel = lax.all_gather(piece, 'col', axis=0, tiled=True)  34.5 us
    pallas_call x2, Pallas kernels, update(): pl.pallas_call(functools.partial(update_kernel, leaving), in_specs=[smem,...  22.8 us
    ppermute x20, starting transfers between devices, send(): lax.ppermute(x, ('col', 'row'), [(a[1] * 2 + a[0], b[1] * 2 + b[0]) for a...  15.7 us
    pallas_call x1, Pallas kernels, place_received(): pl.pallas_call(place_kernel, in_specs=[smem, hbm, hbm, hbm], out_specs=hb...  5.81 us
  transfers between devices with their start and end apart: 21, of which 4 were waited for; matrix products, arithmetic and copies ran while one was open for 2% of the time, Pallas kernels for 24%

profile of v3, /device:TPU:1, one launch (start us, length us, event | category | flops | bytes accessed | tf_op | source)
XLA Modules:
  0.0 201.4 jit_solution(8341155796660907272)
XLA Ops:
  7.2 2.4 %transpose_top.1 = (f32[256,768]{1,0:T(8,128)}, f32[128,768]{1,0:T(8,128)}) custom-call(f32[8192,256]{1,0:T(8,128)} %front_ref.3), custom_call_target="tpu_custom_call" | custom-call | tf_op jit(solution)/shard_map/transpose_top/pallas_call | solution.py:59
  9.6 1.3 collective-permute-start.1
  10.9 1.3 collective-permute-start.2
  12.2 2.1 %collective-permute-done.1 = f32[256,768]{1,0:T(8,128)S(1)} collective-permute-done((f32[256,768]{1,0:T(8,128)}, f32[256,768]{1,0:T(8,128)S(1)}, u32[]{:S(2)}, u32[]{:S(2)}) %collective-permute-start.1) | collective-permute-done | bytes 786464 | tf_op jit(solution)/shard_map/ppermute | solution.py:36
  14.4 8.7 %collective-permute-done.2 = f32[128,768]{1,0:T(8,128)S(1)} collective-permute-done((f32[128,768]{1,0:T(8,128)}, f32[128,768]{1,0:T(8,128)S(1)}, u32[]{:S(2)}, u32[]{:S(2)}) %collective-permute-start.2) | collective-permute-done | bytes 393248 | tf_op jit(solution)/shard_map/ppermute | solution.py:36
  23.1 0.8 slice_select_fusion
  24.1 0.7 collective-permute-start.3
  24.8 0.7 collective-permute-start.9
  25.5 0.7 collective-permute-start.4
  26.2 0.7 collective-permute-start.5
  26.8 0.7 collective-permute-start.10
  27.5 0.7 collective-permute-start.11
  28.4 0.7 collective-permute-start.6
  29.2 0.7 collective-permute-start.12
  29.8 0.7 collective-permute-start.7
  30.5 0.7 collective-permute-start.8
  31.2 0.7 collective-permute-start.13
  31.9 0.7 collective-permute-start.14
  32.8 0.7 collective-permute-start.15
  33.5 0.7 collective-permute-start.17
  34.3 0.7 collective-permute-start.16
  35.0 0.7 collective-permute-start.18
  36.1 1.5 collective-permute-start.19
  37.6 0.7 pad_add_fusion.info_ref
  38.3 53.2 %collective-permute-done.19 = f32[3,512,256]{2,1,0:T(8,128)S(1)} collective-permute-done((f32[3,512,256]{2,1,0:T(8,128)S(1)}, f32[3,512,256]{2,1,0:T(8,128)S(1)}, u32[]{:S(2)}, u32[]{:S(2)}) %collective-permute-start.19) | collective-permute-done | bytes 1572896 | tf_op jit(solution)/shard_map/ppermute | solution.py:36
  91.4 1.3 broadcast_select_fusion.blocks_ref
  92.8 36.5 %solve.1 = (bf16[768,256]{1,0:T(8,128)(2,1)}, bf16[768,256]{1,0:T(8,128)(2,1)}, s32[256]{0:T(256)}) custom-call(s32[2]{0:T(128)} %pad_add_fusion.info_ref, s32[128]{0:T(128)} %map_ref.5, f32[3,512,256]{2,1,0:T(8,128)} %broadcast_select_fusion.blocks_ref, f32[256,768]{1,0:T(8,128)} %copy-done.1), custom_call_target="tpu_custom_call" | custom-call | flops 8000000000 | bytes 100000000 | tf_op jit(solution)/shard_map/solve/pallas_call | solution.py:180
  129.3 34.5 %all-gather.2.cloned.1.call-done.panel_ref = f32[8192,768]{1,0:T(8,128)} async-done(((f32[128,768]{1,0:T(8,128)}), f32[8192,768]{1,0:T(8,128)}) %all-gather.2.cloned.1.call-update) | async-done | bytes 25165840 | tf_op jit(solution)/shard_map/all_gather | solution.py:408
  163.8 11.4 %update_leaving.1 = (f32[8192,256]{1,0:T(8,128)}, f32[5120,256]{1,0:T(8,128)}, f32[3072,256]{1,0:T(8,128)S(1)}) custom-call(s32[2]{0:T(128)} %pad_add_fusion.info_ref, s32[128]{0:T(128)} %map_ref.5, s32[256]{0:T(256)} %get-tuple-element.23.plan_ref, f32[8192,768]{1,0:T(8,128)} %all-gather.2.cloned.1.call-done.panel_ref, f32[8192,256]{1,0:T(8,128)} %front_ref.3, ...), custom_call_target="tpu_custom_call" | custom-call | flops 4800000000 | bytes 32000000 | tf_op jit(solution)/shard_map/update_leaving/pallas_call | solution.py:328
  175.2 0.8 collective-permute-start.20
  177.3 11.4 %update_staying.1 = (f32[8192,256]{1,0:T(8,128)}, f32[8192,256]{1,0:T(8,128)}) custom-call(s32[2]{0:T(128)} %pad_add_fusion.info_ref, s32[128]{0:T(128)} %map_ref.5, s32[256]{0:T(256)} %get-tuple-element.23.plan_ref, f32[8192,768]{1,0:T(8,128)} %all-gather.2.cloned.1.call-done.panel_ref, f32[8192,256]{1,0:T(8,128)} %front_ref.3, ...), custom_call_target="tpu_custom_call", output_to_operand_aliasing={{0}: (7, {})} | custom-call | flops 4800000000 | bytes 32000000 | tf_op jit(solution)/shard_map/update_staying/pallas_call | solution.py:328
  188.7 5.8 %place_received.1 = f32[8192,256]{1,0:T(8,128)} custom-call(s32[256]{0:T(256)} %get-tuple-element.23.plan_ref, f32[5120,256]{1,0:T(8,128)} %collective-permute-done.20.got1_ref, f32[3072,256]{1,0:T(8,128)S(1)} %get-tuple-element.36.got2_ref, f32[8192,256]{1,0:T(8,128)} %get-tuple-element.30._), custom_call_target="tpu_custom_call", output_to_operand_aliasing={{}: (3, {})} | custom-call | tf_op jit(solution)/shard_map/place_received/pallas_call | solution.py:379
  (42 shorter events, 1.6 us)
Async XLA Ops:
  7.2 156.6 %all-gather.2.cloned.1.call-start = ((), (), s32[]{:S(2)}) async-start(), calls=%async_computation | async-start | bytes 25559040 | tf_op jit(solution)/shard_map/all_gather | solution.py:408
  9.6 4.7 %collective-permute-start.1 = (f32[256,768]{1,0:T(8,128)}, f32[256,768]{1,0:T(8,128)S(1)}, u32[]{:S(2)}, u32[]{:S(2)}) collective-permute-start(f32[256,768]{1,0:T(8,128)} %get-tuple-element.22), channel_id=1, source_target_pairs={{0,1},{2,3},{4,5},{6,7},{8,9},{10,11},{12,13},{14,15},{16,17},{18,... | collective-permute-start | bytes 2359304 | tf_op jit(solution)/shard_map/ppermute | solution.py:36
  10.9 12.2 %collective-permute-start.2 = (f32[128,768]{1,0:T(8,128)}, f32[128,768]{1,0:T(8,128)S(1)}, u32[]{:S(2)}, u32[]{:S(2)}) collective-permute-start(f32[128,768]{1,0:T(8,128)} %get-tuple-element.20), channel_id=1, source_target_pairs={{0,96},{2,98},{4,100},{6,102},{8,104},{10,106},{12,108},{14,110},{... | collective-permute-start | bytes 1179656 | tf_op jit(solution)/shard_map/ppermute | solution.py:36
  14.4 9.6 %copy-start.1 = (f32[256,768]{1,0:T(8,128)}, f32[256,768]{1,0:T(8,128)S(1)}, u32[]{:S(2)}) copy-start(f32[256,768]{1,0:T(8,128)S(1)} %broadcast_select_fusion.1.rhs_ref) | copy-start | bytes 2359300
  14.4 9.6 %slice-start = ((f32[8192,256]{1,0:T(8,128)}), f32[768,256]{1,0:T(8,128)S(1)}, s32[]{:S(2)}) async-start(f32[8192,256]{1,0:T(8,128)} %front_ref.3), calls=%async_computation.1 | async-start | bytes 1572864 | tf_op jit(solution)/shard_map/slice | solution.py:410
  14.4 9.6 %copy-start = (f32[256,768]{1,0:T(8,128)S(1)}, f32[256,768]{1,0:T(8,128)}, u32[]{:S(2)}) copy-start(f32[256,768]{1,0:T(8,128)} %get-tuple-element.22) | copy-start | bytes 2359300
  24.1 2.1 %collective-permute-start.3 = (f32[256,256]{1,0:T(8,128)S(1)}, f32[256,256]{1,0:T(8,128)S(1)}, u32[]{:S(2)}, u32[]{:S(2)}) collective-permute-start(f32[256,256]{1,0:T(8,128)S(1)} %get-tuple-element.34), channel_id=1, source_target_pairs={{0,8},{2,10},{4,12}} | collective-permute-start | bytes 786440 | tf_op jit(solution)/shard_map/ppermute | solution.py:36
  24.8 2.8 %collective-permute-start.9 = (f32[256,256]{1,0:T(8,128)S(1)}, f32[256,256]{1,0:T(8,128)S(1)}, u32[]{:S(2)}, u32[]{:S(2)}) collective-permute-start(f32[256,256]{1,0:T(8,128)S(1)} %get-tuple-element.35), channel_id=1, source_target_pairs={{0,32},{2,34},{4,36}} | collective-permute-start | bytes 786440 | tf_op jit(solution)/shard_map/ppermute | solution.py:36
  25.5 2.8 %collective-permute-start.4 = (f32[256,256]{1,0:T(8,128)S(1)}, f32[256,256]{1,0:T(8,128)S(1)}, u32[]{:S(2)}, u32[]{:S(2)}) collective-permute-start(f32[256,256]{1,0:T(8,128)S(1)} %get-tuple-element.34), channel_id=1, source_target_pairs={{0,24},{2,26},{4,28}} | collective-permute-start | bytes 786440 | tf_op jit(solution)/shard_map/ppermute | solution.py:36
  26.2 2.1 %collective-permute-start.5 = (f32[256,256]{1,0:T(8,128)S(1)}, f32[256,256]{1,0:T(8,128)S(1)}, u32[]{:S(2)}, u32[]{:S(2)}) collective-permute-start(f32[256,256]{1,0:T(8,128)S(1)} %collective-permute-done.3), channel_id=1, source_target_pairs={{8,16},{10,18},{12,20}} | collective-permute-start | bytes 786440 | tf_op jit(solution)/shard_map/ppermute | solution.py:36
  26.8 2.2 %collective-permute-start.10 = (f32[256,256]{1,0:T(8,128)S(1)}, f32[256,256]{1,0:T(8,128)S(1)}, u32[]{:S(2)}, u32[]{:S(2)}) collective-permute-start(f32[256,256]{1,0:T(8,128)S(1)} %get-tuple-element.35), channel_id=1, source_target_pairs={{0,96},{2,98},{4,100}} | collective-permute-start | bytes 786440 | tf_op jit(solution)/shard_map/ppermute | solution.py:36
  27.5 1.5 collective-permute-start.11
  28.4 2.2 %collective-permute-start.6 = (f32[256,256]{1,0:T(8,128)S(1)}, f32[256,256]{1,0:T(8,128)S(1)}, u32[]{:S(2)}, u32[]{:S(2)}) collective-permute-start(f32[256,256]{1,0:T(8,128)S(1)} %select_select_fusion.4), channel_id=1, source_target_pairs={{0,32},{2,34},{4,36},{8,40},{10,42},{12,44},{16,48},{18,50},{20,52... | collective-permute-start | bytes 786440 | tf_op jit(solution)/shard_map/ppermute | solution.py:36
  29.2 2.8 %collective-permute-start.12 = (f32[256,256]{1,0:T(8,128)S(1)}, f32[256,256]{1,0:T(8,128)S(1)}, u32[]{:S(2)}, u32[]{:S(2)}) collective-permute-start(f32[256,256]{1,0:T(8,128)S(1)} %select_select_fusion.1), channel_id=1, source_target_pairs={{0,8},{2,10},{4,12},{32,40},{34,42},{36,44},{64,72},{66,74},{68,76... | collective-permute-start | bytes 786440 | tf_op jit(solution)/shard_map/ppermute | solution.py:36
  29.8 2.8 %collective-permute-start.7 = (f32[256,256]{1,0:T(8,128)S(1)}, f32[256,256]{1,0:T(8,128)S(1)}, u32[]{:S(2)}, u32[]{:S(2)}) collective-permute-start(f32[256,256]{1,0:T(8,128)S(1)} %select_select_fusion.4), channel_id=1, source_target_pairs={{0,96},{2,98},{4,100},{8,104},{10,106},{12,108},{16,112},{18,114},... | collective-permute-start | bytes 786440 | tf_op jit(solution)/shard_map/ppermute | solution.py:36
  30.5 2.1 %collective-permute-start.8 = (f32[256,256]{1,0:T(8,128)S(1)}, f32[256,256]{1,0:T(8,128)S(1)}, u32[]{:S(2)}, u32[]{:S(2)}) collective-permute-start(f32[256,256]{1,0:T(8,128)S(1)} %collective-permute-done.6), channel_id=1, source_target_pairs={{32,64},{34,66},{36,68},{40,72},{42,74},{44,76},{48,80},{50,82},{5... | collective-permute-start | bytes 786440 | tf_op jit(solution)/shard_map/ppermute | solution.py:36
  31.2 1.5 collective-permute-start.13
  31.9 0.8 collective-permute-start.14
  32.8 1.4 collective-permute-start.15
  33.5 1.4 collective-permute-start.17
  34.3 1.5 collective-permute-start.16
  35.0 0.8 collective-permute-start.18
  36.1 55.3 %collective-permute-start.19 = (f32[3,512,256]{2,1,0:T(8,128)S(1)}, f32[3,512,256]{2,1,0:T(8,128)S(1)}, u32[]{:S(2)}, u32[]{:S(2)}) collective-permute-start(f32[3,512,256]{2,1,0:T(8,128)S(1)} %pad_maximum_fusion), channel_id=1, source_target_pairs={{0,1},{2,3},{4,5},{6,7},{8,9},{10,11},{12,13},{14,15},{16,17},{18,... | collective-permute-start | bytes 4718600 | tf_op jit(solution)/shard_map/ppermute | solution.py:36
  163.8 12.2 %copy-start.2 = (s32[128]{0:T(128)S(1)}, s32[128]{0:T(128)}, u32[]{:S(2)}) copy-start(s32[128]{0:T(128)} %map_ref.5) | copy-start | bytes 1540
  175.2 13.5 %collective-permute-start.20 = (f32[5120,256]{1,0:T(8,128)}, f32[5120,256]{1,0:T(8,128)}, u32[]{:S(2)}, u32[]{:S(2)}) collective-permute-start(f32[5120,256]{1,0:T(8,128)} %get-tuple-element.28), channel_id=1, source_target_pairs={{0,1},{2,3},{4,5},{6,7},{8,9},{10,11},{12,13},{14,15},{16,17},{18,... | collective-permute-start | bytes 15728648 | tf_op jit(solution)/shard_map/ppermute | solution.py:36
Sparse Core Ops, SparseCore 0:
  24.1 139.6 all-gather.1

commit v4 on v3

--- a/solution.py
+++ b/solution.py
@@ -16,6 +16,7 @@
 GROUP = 4
 SLOTS = 4
 FIRST = 40
+CHUNK = 8
 HIGHEST = lax.Precision.HIGHEST
 VMEM_LIMIT = 56 * 1024 * 1024
 
@@ -346,31 +347,35 @@
 
 
 def place_kernel(plan_ref, got1_ref, got2_ref, _, parent_ref, buf, in_sem, out_sem):
-    def read1(n):
-        return pltpu.make_async_copy(block(got1_ref, n), buf.at[n], in_sem.at[n])
-
-    def read2(n):
-        return pltpu.make_async_copy(block(got2_ref, n - FIRST), buf.at[n], in_sem.at[n])
+    count = plan_ref[3 * HALF + 2]
+
+    def read(i):
+        rows = CHUNK * B
+        source, at = (got1_ref, i) if i * CHUNK < FIRST else (got2_ref, i - FIRST // CHUNK)
+        return pltpu.make_async_copy(source.at[pl.ds(at * rows, rows), :], buf.at[pl.ds(i * rows, rows), :], in_sem.at[i])
 
     def write(n):
-        return pltpu.make_async_copy(buf.at[n], block(parent_ref, plan_ref[2 * HALF + n]), out_sem.at[n])
-
-    def each(first, last, act):
-        @pl.loop(first, last)
-        def _(n):
-            act(n)
-
-    def pass_on(copy, n):
-        copy.wait()
-        write(n).start()
-
-    count = plan_ref[3 * HALF + 2]
-    split = jnp.minimum(count, FIRST)
-    each(0, split, lambda n: read1(n).start())
-    each(split, count, lambda n: read2(n).start())
-    each(0, split, lambda n: pass_on(read1(n), n))
-    each(split, count, lambda n: pass_on(read2(n), n))
-    each(0, count, lambda n: write(n).wait())
+        return pltpu.make_async_copy(block(buf, n), block(parent_ref, plan_ref[2 * HALF + n]), out_sem.at[n])
+
+    for i in range(HALF // CHUNK):
+
+        @pl.when(i * CHUNK < count)
+        def _():
+            read(i).start()
+
+    for i in range(HALF // CHUNK):
+
+        @pl.when(i * CHUNK < count)
+        def _():
+            read(i).wait()
+
+            @pl.loop(i * CHUNK, jnp.minimum(count, (i + 1) * CHUNK))
+            def _(n):
+                write(n).start()
+
+    @pl.loop(0, count)
+    def _(n):
+        write(n).wait()
 
 
 def place_received(lists, got1, got2, parent):
@@ -383,8 +388,8 @@
         out_shape=jax.ShapeDtypeStruct(parent.shape, jnp.float32),
         input_output_aliases={3: 0},
         scratch_shapes=[
-            pltpu.VMEM((HALF, B, W), jnp.float32),
-            pltpu.SemaphoreType.DMA((HALF,)),
+            pltpu.VMEM((HALF * B, W), jnp.float32),
+            pltpu.SemaphoreType.DMA((HALF // CHUNK,)),
             pltpu.SemaphoreType.DMA((HALF,)),
         ],
         compiler_params=pltpu.CompilerParams(vmem_limit_bytes=VMEM_LIMIT),
@@ -433,11 +438,12 @@
     blocks = jnp.where(r == 0, blocks, blocks_down)
     hi, lo, lists = solve(info, row_map, blocks, mine)
 
+    many = jnp.sum((row_map[:HALF] >= HALF).astype(jnp.int32)) > FIRST
+    hi, many = lax.optimization_barrier((hi, many))
     factored, send1, send2 = update(True, info, row_map, lists, panel, front, hi, lo)
     swap = [((i, k), (1 - i, k)) for i in range(2) for k in range(COLS)]
     got1 = send(send1, swap)
     factored, parent = update(False, info, row_map, lists, panel, front, hi, lo, factored)
-    many = jnp.sum((row_map[:HALF] >= HALF).astype(jnp.int32)) > FIRST
     got2 = lax.cond(many, lambda v: send(v, swap), lambda v: v, send2)
     parent = place_received(lists, got1, got2, parent)
     return factored, parent

time: 202 us -> 199 us (0.985)
  waiting for transfers between devices: 98.4 us -> 95.9 us
where the time goes in v4:
time: 199 us
  waiting for transfers between devices  95.9 us (48%)
  Pallas kernels  66.3 us (33%)
  starting transfers between devices  15.7 us (8%)
  between operations  15.3 us (8%)
  other arithmetic  5.45 us (3%)
    ppermute x20, waiting for transfers between devices, send(): lax.ppermute(x, ('col', 'row'), [(a[1] * 2 + a[0], b[1] * 2 + b[0]) for a...  62.8 us
    pallas_call x1, Pallas kernels, solve(): pl.pallas_call(solve_kernel, in_specs=[smem, smem, vmem, vmem], out_specs...  36.5 us
    all_gather x1, waiting for transfers between devices, per_device(): panel = lax.all_gather(piece, 'col', axis=0, tiled=True)  33.1 us
    pallas_call x2, Pallas kernels, update(): pl.pallas_call(functools.partial(update_kernel, leaving), in_specs=[smem,...  22.8 us
    ppermute x20, starting transfers between devices, send(): lax.ppermute(x, ('col', 'row'), [(a[1] * 2 + a[0], b[1] * 2 + b[0]) for a...  15.7 us
    pallas_call x1, Pallas kernels, place_received(): pl.pallas_call(place_kernel, in_specs=[smem, hbm, hbm, hbm], out_specs=hb...  4.54 us
  transfers between devices with their start and end apart: 21, of which 4 were waited for; matrix products, arithmetic and copies ran while one was open for 2% of the time, Pallas kernels for 24%

profile of v4, /device:TPU:1, one launch (start us, length us, event | category | flops | bytes accessed | tf_op | source)
XLA Modules:
  0.0 198.8 jit_solution(12624766325364224672)
XLA Ops:
  7.2 2.4 %transpose_top.1 = (f32[256,768]{1,0:T(8,128)}, f32[128,768]{1,0:T(8,128)}) custom-call(f32[8192,256]{1,0:T(8,128)} %front_ref.3), custom_call_target="tpu_custom_call" | custom-call | tf_op jit(solution)/shard_map/transpose_top/pallas_call | solution.py:60
  9.6 1.3 collective-permute-start.1
  10.9 1.3 collective-permute-start.2
  12.2 2.1 %collective-permute-done.1 = f32[256,768]{1,0:T(8,128)S(1)} collective-permute-done((f32[256,768]{1,0:T(8,128)}, f32[256,768]{1,0:T(8,128)S(1)}, u32[]{:S(2)}, u32[]{:S(2)}) %collective-permute-start.1) | collective-permute-done | bytes 786464 | tf_op jit(solution)/shard_map/ppermute | solution.py:37
  14.4 8.7 %collective-permute-done.2 = f32[128,768]{1,0:T(8,128)S(1)} collective-permute-done((f32[128,768]{1,0:T(8,128)}, f32[128,768]{1,0:T(8,128)S(1)}, u32[]{:S(2)}, u32[]{:S(2)}) %collective-permute-start.2) | collective-permute-done | bytes 393248 | tf_op jit(solution)/shard_map/ppermute | solution.py:37
  23.1 0.8 slice_select_fusion
  24.1 0.7 collective-permute-start.3
  24.8 0.7 collective-permute-start.9
  25.5 0.7 collective-permute-start.4
  26.2 0.7 collective-permute-start.5
  26.8 0.7 collective-permute-start.10
  27.5 0.7 collective-permute-start.11
  28.4 0.7 collective-permute-start.6
  29.2 0.7 collective-permute-start.12
  29.8 0.7 collective-permute-start.7
  30.5 0.7 collective-permute-start.8
  31.2 0.7 collective-permute-start.13
  31.9 0.7 collective-permute-start.14
  32.8 0.7 collective-permute-start.15
  33.5 0.7 collective-permute-start.17
  34.3 0.7 collective-permute-start.16
  36.0 1.2 pad_maximum_fusion
  37.3 1.5 collective-permute-start.19
  38.8 0.7 fusion
  40.8 52.0 %collective-permute-done.19 = f32[3,512,256]{2,1,0:T(8,128)S(1)} collective-permute-done((f32[3,512,256]{2,1,0:T(8,128)}, f32[3,512,256]{2,1,0:T(8,128)S(1)}, u32[]{:S(2)}, u32[]{:S(2)}) %collective-permute-start.19) | collective-permute-done | bytes 1572896 | tf_op jit(solution)/shard_map/ppermute | solution.py:37
  92.8 1.3 broadcast_select_fusion.blocks_ref
  94.1 36.5 %solve.1 = (bf16[768,256]{1,0:T(8,128)(2,1)}, bf16[768,256]{1,0:T(8,128)(2,1)}, s32[256]{0:T(256)}) custom-call(s32[2]{0:T(128)} %pad_add_fusion.info_ref, s32[128]{0:T(128)} %map_ref.5, f32[3,512,256]{2,1,0:T(8,128)} %broadcast_select_fusion.blocks_ref, f32[256,768]{1,0:T(8,128)} %copy-done.1), custom_call_target="tpu_custom_call" | custom-call | flops 8000000000 | bytes 100000000 | tf_op jit(solution)/shard_map/solve/pallas_call | solution.py:181
  130.7 33.1 %all-gather.2.cloned.1.call-done.panel_ref = f32[8192,768]{1,0:T(8,128)} async-done(((f32[128,768]{1,0:T(8,128)}), f32[8192,768]{1,0:T(8,128)}) %all-gather.2.cloned.1.call-update) | async-done | bytes 25165840 | tf_op jit(solution)/shard_map/all_gather | solution.py:413
  163.8 11.4 %update_leaving.1 = (f32[8192,256]{1,0:T(8,128)}, f32[5120,256]{1,0:T(8,128)}, f32[3072,256]{1,0:T(8,128)S(1)}) custom-call(s32[2]{0:T(128)} %pad_add_fusion.info_ref, s32[128]{0:T(128)} %map_ref.5, s32[256]{0:T(256)} %get-tuple-element.25.plan_ref, f32[8192,768]{1,0:T(8,128)} %all-gather.2.cloned.1.call-done.panel_ref, f32[8192,256]{1,0:T(8,128)} %front_ref.3, ...), custom_call_target="tpu_custom_call" | custom-call | flops 4800000000 | bytes 32000000 | tf_op jit(solution)/shard_map/update_leaving/pallas_call | solution.py:329
  175.2 0.8 collective-permute-start.20
  176.0 11.4 %update_staying.1 = (f32[8192,256]{1,0:T(8,128)}, f32[8192,256]{1,0:T(8,128)}) custom-call(s32[2]{0:T(128)} %pad_add_fusion.info_ref, s32[128]{0:T(128)} %map_ref.5, s32[256]{0:T(256)} %get-tuple-element.25.plan_ref, f32[8192,768]{1,0:T(8,128)} %all-gather.2.cloned.1.call-done.panel_ref, f32[8192,256]{1,0:T(8,128)} %front_ref.3, ...), custom_call_target="tpu_custom_call", output_to_operand_aliasing={{0}: (7, {})} | custom-call | flops 4800000000 | bytes 32000000 | tf_op jit(solution)/shard_map/update_staying/pallas_call | solution.py:329
  187.4 4.5 %place_received.1 = f32[8192,256]{1,0:T(8,128)} custom-call(s32[256]{0:T(256)} %get-tuple-element.25.plan_ref, f32[5120,256]{1,0:T(8,128)} %collective-permute-done.20.got1_ref, f32[3072,256]{1,0:T(8,128)S(1)} %get-tuple-element.40.got2_ref, f32[8192,256]{1,0:T(8,128)} %get-tuple-element.34._), custom_call_target="tpu_custom_call", output_to_operand_aliasing={{}: (3, {})} | custom-call | tf_op jit(solution)/shard_map/place_received/pallas_call | solution.py:384
  (42 shorter events, 2.2 us)
Async XLA Ops:
  7.2 156.6 %all-gather.2.cloned.1.call-start = ((), (), s32[]{:S(2)}) async-start(), calls=%async_computation | async-start | bytes 25559040 | tf_op jit(solution)/shard_map/all_gather | solution.py:413
  9.6 4.7 %collective-permute-start.1 = (f32[256,768]{1,0:T(8,128)}, f32[256,768]{1,0:T(8,128)S(1)}, u32[]{:S(2)}, u32[]{:S(2)}) collective-permute-start(f32[256,768]{1,0:T(8,128)} %get-tuple-element.24), channel_id=1, source_target_pairs={{0,1},{2,3},{4,5},{6,7},{8,9},{10,11},{12,13},{14,15},{16,17},{18,... | collective-permute-start | bytes 2359304 | tf_op jit(solution)/shard_map/ppermute | solution.py:37
  10.9 12.2 %collective-permute-start.2 = (f32[128,768]{1,0:T(8,128)}, f32[128,768]{1,0:T(8,128)S(1)}, u32[]{:S(2)}, u32[]{:S(2)}) collective-permute-start(f32[128,768]{1,0:T(8,128)} %get-tuple-element.22), channel_id=1, source_target_pairs={{0,96},{2,98},{4,100},{6,102},{8,104},{10,106},{12,108},{14,110},{... | collective-permute-start | bytes 1179656 | tf_op jit(solution)/shard_map/ppermute | solution.py:37
  14.4 9.6 %copy-start.1 = (f32[256,768]{1,0:T(8,128)}, f32[256,768]{1,0:T(8,128)S(1)}, u32[]{:S(2)}) copy-start(f32[256,768]{1,0:T(8,128)S(1)} %broadcast_select_fusion.1.rhs_ref) | copy-start | bytes 2359300
  14.4 9.6 %slice-start = ((f32[8192,256]{1,0:T(8,128)}), f32[768,256]{1,0:T(8,128)S(1)}, s32[]{:S(2)}) async-start(f32[8192,256]{1,0:T(8,128)} %front_ref.3), calls=%async_computation.1 | async-start | bytes 1572864 | tf_op jit(solution)/shard_map/slice | solution.py:415
  14.4 9.6 %copy-start = (f32[256,768]{1,0:T(8,128)S(1)}, f32[256,768]{1,0:T(8,128)}, u32[]{:S(2)}) copy-start(f32[256,768]{1,0:T(8,128)} %get-tuple-element.24) | copy-start | bytes 2359300
  24.1 2.1 %collective-permute-start.3 = (f32[256,256]{1,0:T(8,128)S(1)}, f32[256,256]{1,0:T(8,128)S(1)}, u32[]{:S(2)}, u32[]{:S(2)}) collective-permute-start(f32[256,256]{1,0:T(8,128)S(1)} %get-tuple-element.38), channel_id=1, source_target_pairs={{0,8},{2,10},{4,12}} | collective-permute-start | bytes 786440 | tf_op jit(solution)/shard_map/ppermute | solution.py:37
  24.8 2.8 %collective-permute-start.9 = (f32[256,256]{1,0:T(8,128)S(1)}, f32[256,256]{1,0:T(8,128)S(1)}, u32[]{:S(2)}, u32[]{:S(2)}) collective-permute-start(f32[256,256]{1,0:T(8,128)S(1)} %get-tuple-element.39), channel_id=1, source_target_pairs={{0,32},{2,34},{4,36}} | collective-permute-start | bytes 786440 | tf_op jit(solution)/shard_map/ppermute | solution.py:37
  25.5 2.8 %collective-permute-start.4 = (f32[256,256]{1,0:T(8,128)S(1)}, f32[256,256]{1,0:T(8,128)S(1)}, u32[]{:S(2)}, u32[]{:S(2)}) collective-permute-start(f32[256,256]{1,0:T(8,128)S(1)} %get-tuple-element.38), channel_id=1, source_target_pairs={{0,24},{2,26},{4,28}} | collective-permute-start | bytes 786440 | tf_op jit(solution)/shard_map/ppermute | solution.py:37
  26.2 2.1 %collective-permute-start.5 = (f32[256,256]{1,0:T(8,128)S(1)}, f32[256,256]{1,0:T(8,128)S(1)}, u32[]{:S(2)}, u32[]{:S(2)}) collective-permute-start(f32[256,256]{1,0:T(8,128)S(1)} %collective-permute-done.3), channel_id=1, source_target_pairs={{8,16},{10,18},{12,20}} | collective-permute-start | bytes 786440 | tf_op jit(solution)/shard_map/ppermute | solution.py:37
  26.8 2.2 %collective-permute-start.10 = (f32[256,256]{1,0:T(8,128)S(1)}, f32[256,256]{1,0:T(8,128)S(1)}, u32[]{:S(2)}, u32[]{:S(2)}) collective-permute-start(f32[256,256]{1,0:T(8,128)S(1)} %get-tuple-element.39), channel_id=1, source_target_pairs={{0,96},{2,98},{4,100}} | collective-permute-start | bytes 786440 | tf_op jit(solution)/shard_map/ppermute | solution.py:37
  27.5 1.5 collective-permute-start.11
  28.4 2.2 %collective-permute-start.6 = (f32[256,256]{1,0:T(8,128)S(1)}, f32[256,256]{1,0:T(8,128)S(1)}, u32[]{:S(2)}, u32[]{:S(2)}) collective-permute-start(f32[256,256]{1,0:T(8,128)S(1)} %select_select_fusion.4), channel_id=1, source_target_pairs={{0,32},{2,34},{4,36},{8,40},{10,42},{12,44},{16,48},{18,50},{20,52... | collective-permute-start | bytes 786440 | tf_op jit(solution)/shard_map/ppermute | solution.py:37
  29.2 2.8 %collective-permute-start.12 = (f32[256,256]{1,0:T(8,128)S(1)}, f32[256,256]{1,0:T(8,128)S(1)}, u32[]{:S(2)}, u32[]{:S(2)}) collective-permute-start(f32[256,256]{1,0:T(8,128)S(1)} %select_select_fusion.1), channel_id=1, source_target_pairs={{0,8},{2,10},{4,12},{32,40},{34,42},{36,44},{64,72},{66,74},{68,76... | collective-permute-start | bytes 786440 | tf_op jit(solution)/shard_map/ppermute | solution.py:37
  29.8 2.8 %collective-permute-start.7 = (f32[256,256]{1,0:T(8,128)S(1)}, f32[256,256]{1,0:T(8,128)S(1)}, u32[]{:S(2)}, u32[]{:S(2)}) collective-permute-start(f32[256,256]{1,0:T(8,128)S(1)} %select_select_fusion.4), channel_id=1, source_target_pairs={{0,96},{2,98},{4,100},{8,104},{10,106},{12,108},{16,112},{18,114},... | collective-permute-start | bytes 786440 | tf_op jit(solution)/shard_map/ppermute | solution.py:37
  30.5 2.1 %collective-permute-start.8 = (f32[256,256]{1,0:T(8,128)S(1)}, f32[256,256]{1,0:T(8,128)S(1)}, u32[]{:S(2)}, u32[]{:S(2)}) collective-permute-start(f32[256,256]{1,0:T(8,128)S(1)} %collective-permute-done.6), channel_id=1, source_target_pairs={{32,64},{34,66},{36,68},{40,72},{42,74},{44,76},{48,80},{50,82},{5... | collective-permute-start | bytes 786440 | tf_op jit(solution)/shard_map/ppermute | solution.py:37
  31.2 1.5 collective-permute-start.13
  31.9 0.8 collective-permute-start.14
  32.8 1.4 collective-permute-start.15
  33.5 1.4 collective-permute-start.17
  34.3 1.5 collective-permute-start.16
  35.0 0.8 collective-permute-start.18
  36.0 2.7 %copy-start.2 = (s32[128]{0:T(128)S(1)}, s32[128]{0:T(128)}, u32[]{:S(2)}) copy-start(s32[128]{0:T(128)} %map_ref.5) | copy-start | bytes 1540
  37.3 55.5 %collective-permute-start.19 = (f32[3,512,256]{2,1,0:T(8,128)}, f32[3,512,256]{2,1,0:T(8,128)S(1)}, u32[]{:S(2)}, u32[]{:S(2)}) collective-permute-start(f32[3,512,256]{2,1,0:T(8,128)} %pad_maximum_fusion), channel_id=1, source_target_pairs={{0,1},{2,3},{4,5},{6,7},{8,9},{10,11},{12,13},{14,15},{16,17},{18,... | collective-permute-start | bytes 4718600 | tf_op jit(solution)/shard_map/ppermute | solution.py:37
  175.2 12.2 %collective-permute-start.20 = (f32[5120,256]{1,0:T(8,128)}, f32[5120,256]{1,0:T(8,128)}, u32[]{:S(2)}, u32[]{:S(2)}) collective-permute-start(f32[5120,256]{1,0:T(8,128)} %get-tuple-element.31), channel_id=1, source_target_pairs={{0,1},{2,3},{4,5},{6,7},{8,9},{10,11},{12,13},{14,15},{16,17},{18,... | collective-permute-start | bytes 15728648 | tf_op jit(solution)/shard_map/ppermute | solution.py:37
Sparse Core Ops, SparseCore 0:
  24.1 139.6 all-gather.1
